TPU v7x, 32 devices: a whole 2x2x4 slice. The times are simulated.
32 devices in a mesh: dp: 4 (over y, core), chan: 2 (over x), seq: 4 (over z).
Axes of the slice: x: 2, y: 2, z: 4, core: 2. Of those that a mesh axis runs over, the one named last changes fastest.
Arguments:
- query_input: bfloat16 [4, 512, 8192], P('dp', 'seq', 'chan'), may hold values from -6 to 6
- key_input: bfloat16 [4, 512, 8192], P('dp', 'seq', 'chan'), may hold values from -6 to 6
- value_input: bfloat16 [4, 512, 8192], P('dp', 'seq', 'chan'), may hold values from -6 to 6
- grad_output: bfloat16 [4, 512, 8192], P('dp', 'seq', 'chan'), may hold values from -6 to 6
- w_embed: float32 [32, 64], replicated, may hold values from -6 to 6
- w_filter: float32 [64, 8192], P(None, ('chan', 'seq')), may hold values from -0.1875 to 0.1875
- decay_rates: float32 [8192], P(('chan', 'seq')), may hold values from 0.1 to 30.72
Outputs:
- d_query: bfloat16 [4, 512, 8192], P('dp', 'seq', 'chan')
- d_key: bfloat16 [4, 512, 8192], P('dp', 'seq', 'chan')
- d_value: bfloat16 [4, 512, 8192], P('dp', 'seq', 'chan')
- grad_filter: float32 [64, 8192], P(None, ('chan', 'seq'))
- grad_rate: float32 [8192], P(('chan', 'seq'))
- grad_embed: float32 [32, 64], replicated
All inputs are finite; a program needn't handle non-finite values.
Results may differ from a plain program's by a relative error of at most 0.0058.
Values may be sent and summed in bfloat16 or wider, within the bound.
A program may use at most 128 MiB of HBM per device.

v0:
```python
import math

import jax
import jax.numpy as jnp
from jax import lax
from jax.sharding import PartitionSpec as P


def embed_features(positions, count, length):
    bands = jnp.arange(count // 2, dtype=jnp.float32) + 0.5
    phase = positions[None, :] * bands[:, None] * (2.0 * math.pi / length)
    return jnp.concatenate([jnp.sin(phase), jnp.cos(phase)], axis=0)


def angle_table(row_count, col_count, period):
    left = jnp.arange(row_count, dtype=jnp.float32)
    right = jnp.arange(col_count, dtype=jnp.float32)
    angles = jnp.outer(left, right) % period * (2.0 * math.pi / period)
    return (jnp.cos(angles), jnp.sin(angles))


def make_tables(half_outer, inner_size, fft_size):
    outer_size = 2 * half_outer
    outer_cos, outer_sin = angle_table(outer_size, outer_size, outer_size)
    twist_cos, twist_sin = angle_table(outer_size, inner_size, fft_size)
    inner_cos, inner_sin = angle_table(inner_size, inner_size, inner_size)
    first_table = jnp.stack([outer_cos[:half_outer], -outer_sin[:half_outer]], axis=1)
    last_forward = jnp.stack(
        [jnp.stack([inner_cos, -inner_sin], axis=1), jnp.stack([inner_sin, inner_cos], axis=1)],
        axis=0,
    )
    last_inverse = jnp.stack(
        [jnp.stack([inner_cos, inner_sin], axis=1), jnp.stack([-inner_sin, inner_cos], axis=1)],
        axis=0,
    )
    cos_head = outer_cos[:, :half_outer]
    sin_head = outer_sin[:, :half_outer]
    middle_both = jnp.stack(
        [jnp.stack([cos_head, sin_head], axis=1), jnp.stack([-sin_head, cos_head], axis=1)], axis=0
    )
    middle_real = jnp.stack([cos_head[:, None], -sin_head[:, None]], axis=0)
    return (first_table, twist_cos, twist_sin, last_forward, last_inverse, middle_both, middle_real)


def forward_spec(signal, tables, half_outer, inner_size):
    first_table, twist_cos, twist_sin, last_forward = (tables[0], tables[1], tables[2], tables[3])
    blocks = signal.reshape(signal.shape[0], half_outer, inner_size)
    first = jnp.einsum("cnm,nqk->cqkm", blocks, first_table, precision=lax.Precision.HIGHEST)
    part_real = first[:, 0]
    part_imag = first[:, 1]
    turned = jnp.stack(
        [
            part_real * twist_cos + part_imag * twist_sin,
            part_imag * twist_cos - part_real * twist_sin,
        ],
        axis=1,
    )
    return jnp.einsum("cpkm,pmqj->cqkj", turned, last_forward, precision=lax.Precision.HIGHEST)


def inverse_head(spec, tables, middle, fft_size):
    twist_cos, twist_sin, last_inverse = (tables[1], tables[2], tables[4])
    back = jnp.einsum("cpkm,pmqj->cqkj", spec, last_inverse, precision=lax.Precision.HIGHEST)
    back_real = back[:, 0]
    back_imag = back[:, 1]
    turned = jnp.stack(
        [
            back_real * twist_cos - back_imag * twist_sin,
            back_real * twist_sin + back_imag * twist_cos,
        ],
        axis=1,
    )
    times = jnp.einsum("cpkm,pkqn->cqnm", turned, middle, precision=lax.Precision.HIGHEST)
    return times.reshape(times.shape[0], times.shape[1], -1) / fft_size


def channel_work(conv_input, conv_upstream, filter_taps, half_outer, inner_size):
    length = conv_input.shape[1]
    fft_size = 2 * length
    tables = make_tables(half_outer, inner_size, fft_size)
    input_spec = forward_spec(conv_input, tables, half_outer, inner_size)
    upstream_spec = forward_spec(conv_upstream, tables, half_outer, inner_size)
    taps_spec = forward_spec(filter_taps, tables, half_outer, inner_size)
    input_real, input_imag = (input_spec[:, 0], input_spec[:, 1])
    upstream_real, upstream_imag = (upstream_spec[:, 0], upstream_spec[:, 1])
    taps_real, taps_imag = (taps_spec[:, 0], taps_spec[:, 1])
    conv_real = taps_real * input_real - taps_imag * input_imag
    conv_imag = taps_real * input_imag + taps_imag * input_real
    grad_real = taps_real * upstream_real + taps_imag * upstream_imag
    grad_imag = taps_real * upstream_imag - taps_imag * upstream_real
    joined = jnp.stack([conv_real - grad_imag, conv_imag + grad_real], axis=1)
    both = inverse_head(joined, tables, tables[5], fft_size)
    corr_real = input_real * upstream_real + input_imag * upstream_imag
    corr_imag = input_real * upstream_imag - input_imag * upstream_real
    correlation = inverse_head(
        jnp.stack([corr_real, corr_imag], axis=1), tables, tables[6], fft_size
    )
    return (both[:, 0], both[:, 1], correlation[:, 0])


def filter_grads(filter_grad, hidden_t, w_filter, window, filter_taps, positions, length):
    time_scale = 1.0 / math.sqrt(length)
    weighted = filter_grad * window
    grad_filter = (
        jnp.einsum("jt,ct->jc", hidden_t, weighted, precision=lax.Precision.HIGHEST) * time_scale
    )
    grad_rate = (
        -jnp.sum(positions[None, :] / length * filter_taps * filter_grad, axis=1) * time_scale
    )
    hidden_grad = jnp.einsum("jc,ct->jt", w_filter, weighted, precision=lax.Precision.HIGHEST)
    return (grad_filter, grad_rate, hidden_grad)


def embed_term(features_t, hidden_grad, pre_t, length):
    return jnp.einsum(
        "et,jt->ej", features_t, hidden_grad * jnp.cos(pre_t), precision=lax.Precision.HIGHEST
    ) * (1.0 / math.sqrt(length))


def per_device(query_input, key_input, value_input, grad_output, w_embed, w_filter, decay_rates):
    seq_count = lax.axis_size("seq")
    batch_count = lax.axis_size("dp")
    local_len = query_input.shape[1]
    length = local_len * seq_count
    query_all, key_all, value_all, grad_all = (
        lax.all_to_all(query_input, "seq", split_axis=2, concat_axis=1, tiled=True),
        lax.all_to_all(key_input, "seq", split_axis=2, concat_axis=1, tiled=True),
        lax.all_to_all(value_input, "seq", split_axis=2, concat_axis=1, tiled=True),
        lax.all_to_all(grad_output, "seq", split_axis=2, concat_axis=1, tiled=True),
    )
    product = (key_all.astype(jnp.float32) * value_all.astype(jnp.float32)).astype(jnp.bfloat16)
    upstream = (grad_all.astype(jnp.float32) * query_all.astype(jnp.float32)).astype(jnp.bfloat16)
    product, upstream = lax.optimization_barrier((product, upstream))
    conv_input = product[0].T.astype(jnp.float32)
    conv_upstream = upstream[0].T.astype(jnp.float32)
    positions = jnp.arange(length, dtype=jnp.float32)
    features_t = embed_features(positions, w_embed.shape[0], length)
    pre_t = jnp.einsum("ej,et->jt", w_embed, features_t, precision=lax.Precision.HIGHEST)
    hidden_t = jnp.sin(pre_t)
    window = jnp.exp(-decay_rates[:, None] * positions[None, :] / length)
    filter_taps = (
        jnp.einsum("jc,jt->ct", w_filter, hidden_t, precision=lax.Precision.HIGHEST) * window
    )
    conv_out, conv_grad, correlation = channel_work(
        conv_input, conv_upstream, filter_taps, seq_count, local_len
    )
    correlation = correlation * (1.0 / math.sqrt(batch_count * length))
    conv_send = conv_out.T[None].astype(jnp.bfloat16)
    grad_send = conv_grad.T[None].astype(jnp.bfloat16)
    conv_send, grad_send = lax.optimization_barrier((conv_send, grad_send))
    conv_wide = conv_send.astype(jnp.float32)
    grad_wide = grad_send.astype(jnp.float32)
    d_query = (grad_all.astype(jnp.float32) * conv_wide).astype(jnp.bfloat16)
    d_key = (grad_wide * value_all.astype(jnp.float32)).astype(jnp.bfloat16)
    d_value = (grad_wide * key_all.astype(jnp.float32)).astype(jnp.bfloat16)
    d_query, d_key, d_value = (
        lax.all_to_all(d_query, "seq", split_axis=1, concat_axis=2, tiled=True),
        lax.all_to_all(d_key, "seq", split_axis=1, concat_axis=2, tiled=True),
        lax.all_to_all(d_value, "seq", split_axis=1, concat_axis=2, tiled=True),
    )
    summed = lax.psum(correlation, "dp")
    grad_filter, grad_rate, hidden_grad = filter_grads(
        summed, hidden_t, w_filter, window, filter_taps, positions, length
    )
    hidden_grad = lax.psum(hidden_grad, ("chan", "seq"))
    grad_embed = embed_term(features_t, hidden_grad, pre_t, length)
    return (d_query, d_key, d_value, grad_filter, grad_rate, grad_embed)


def solution(mesh):
    in_specs = (
        P("dp", "seq", "chan"),
        P("dp", "seq", "chan"),
        P("dp", "seq", "chan"),
        P("dp", "seq", "chan"),
        P(),
        P(None, ("chan", "seq")),
        P(("chan", "seq")),
    )
    out_specs = (
        P("dp", "seq", "chan"),
        P("dp", "seq", "chan"),
        P("dp", "seq", "chan"),
        P(None, ("chan", "seq")),
        P(("chan", "seq")),
        P(),
    )
    return jax.shard_map(
        per_device, mesh=mesh, in_specs=in_specs, out_specs=out_specs, check_vma=False
    )
```

profile of v0, /device:TPU:0, one launch (start us, length us, event | category | flops | bytes accessed | tf_op | source)
XLA Modules:
  0.0 609.4 jit_solution(12989453345135064856)
XLA Ops:
  7.2 5.1 copy.104
  12.9 22.4 %reduce = bf16[4096,128]{1,0:T(8,128)(2,1)S(1)} reduce(bf16[4096,1,128]{2,1,0:T(2,128)(2,1)S(1)} %bitcast.261, bf16[]{:T(256)} %broadcast.196), dimensions={1}, to_apply=%bitcast.215.reduce_sub_computation | reduce | bytes 2097154
  36.9 6.3 %all-to-all-start = ((bf16[4,2,65536]{2,1,0:T(2,128)(2,1)}), bf16[4,2,65536]{2,1,0:T(2,128)(2,1)S(1)}, u32[]{:S(2)}, u32[]{:S(2)}) async-start(bf16[4,2,65536]{2,1,0:T(2,128)(2,1)} %reshape.268), calls=%async_computation | async-start | bytes 2097152 | tf_op jit(solution)/shard_map/all_to_all | solution.py:129
  43.3 5.0 copy.113
  48.3 23.4 %reduce.3 = bf16[4096,128]{1,0:T(8,128)(2,1)} reduce(bf16[4096,1,128]{2,1,0:T(2,128)(2,1)S(1)} %bitcast.269, bf16[]{:T(256)} %broadcast.196), dimensions={1}, to_apply=%bitcast.217.reduce_sub_computation | reduce | bytes 2097154
  71.7 3.5 reshape.270
  76.1 5.6 all-to-all-start.1
  81.7 5.0 copy.115
  86.7 23.4 %reduce.2 = bf16[4096,128]{1,0:T(8,128)(2,1)} reduce(bf16[4096,1,128]{2,1,0:T(2,128)(2,1)S(1)} %bitcast.270, bf16[]{:T(256)} %broadcast.196), dimensions={1}, to_apply=%bitcast.219.reduce_sub_computation | reduce | bytes 2097154
  110.1 3.5 reshape.272
  113.6 5.0 copy.117
  118.7 23.4 %reduce.1 = bf16[4096,128]{1,0:T(8,128)(2,1)} reduce(bf16[4096,1,128]{2,1,0:T(2,128)(2,1)S(1)} %bitcast.271, bf16[]{:T(256)} %broadcast.196), dimensions={1}, to_apply=%bitcast.221.reduce_sub_computation | reduce | bytes 2097154
  142.1 3.5 reshape.274
  148.1 5.3 all-to-all-start.2
  153.3 3.4 bitcast_multiply_fusion.5
  161.4 9.1 %convolution_bitcast_fusion.4 = f32[1024,2,8,128]{3,2,0,1:T(8,128)} fusion(f32[1024,4,128]{2,1,0:T(4,128)S(1)} %copy.111, f32[4,1,8]{2,0,1:T(4,128)S(1)} %bitcast.280, f32[4,1,8]{2,0,1:T(4,128)S(1)} %bitcast.283), kind=kOutput, calls=%fused_computation.45 | convolution fusion | flops 100663360 | bytes 10486016 | tf_op jit(solution)/shard_map/cnm,nqk->cqkm/dot_general | solution.py:48
  173.1 4.9 all-to-all-done.2
  178.0 4.5 all-to-all-start.3
  182.5 3.3 bitcast_convert_fusion.3
  185.8 2.9 copy.105
  189.7 3.3 bitcast_convert_fusion.2
  195.0 4.1 reshape.273
  199.1 4.8 bitcast_convert_fusion.1
  203.9 2.9 copy.116
  207.8 4.1 reshape.275
  211.9 4.8 bitcast_convert_fusion
  216.7 3.0 copy.118
  219.6 4.7 fusion.31
  226.7 6.8 %convolution_bitcast_fusion.2 = f32[1024,2,8,128]{3,2,0,1:T(8,128)} fusion(bf16[1024,4,128]{2,1,0:T(4,128)(2,1)} %copy.121, f32[4,1,8]{2,0,1:T(4,128)S(1)} %bitcast.281, f32[4,1,8]{2,0,1:T(4,128)S(1)} %bitcast.284), kind=kOutput, calls=%fused_computation.43 | convolution fusion | flops 100663360 | bytes 9437440 | tf_op jit(solution)/shard_map/cnm,nqk->cqkm/dot_general | solution.py:48
  234.9 6.7 %convolution_bitcast_fusion.3 = f32[1024,2,8,128]{3,2,0,1:T(8,128)} fusion(bf16[1024,4,128]{2,1,0:T(4,128)(2,1)} %copy.119, f32[4,1,8]{2,0,1:T(4,128)S(1)} %bitcast.282, f32[4,1,8]{2,0,1:T(4,128)S(1)} %bitcast.285), kind=kOutput, calls=%fused_computation.44 | convolution fusion | flops 100663360 | bytes 9437440 | tf_op jit(solution)/shard_map/cnm,nqk->cqkm/dot_general | solution.py:48
  241.7 17.7 %multiply_add_fusion.4 = (f32[1024,1,8,128]{3,2,0,1:T(8,128)}, f32[1024,1,8,128]{3,2,0,1:T(8,128)}, f32[1024,1,8,128]{3,2,0,1:T(8,128)}, f32[1024,1,8,128]{3,2,0...) fusion(f32[1024,2,8,128]{3,2,0,1:T(8,128)} %convolution_bitcast_fusion.3, ...), kind=kLoop, calls=%fused_computation.35 | loop fusion | flops 18874368 | bytes 50339840 | tf_op jit(solution)/shard_map/add | solution.py:53
  259.3 4.0 pad_maximum_fusion
  263.4 4.0 pad_maximum_fusion.1
  267.4 10.5 %fusion.17 = f32[1024,2,8,128]{0,3,2,1:T(8,128)} fusion(f32[1024,2,8,128]{3,2,0,1:T(8,128)S(1)} %pad_maximum_fusion, f32[1,128,2,128]{1,3,0,2:T(8,128)S(1)} %get-tuple-element.39, f32[1,128,2,128]{1,3,0,2:T(8,128)S(1)} %copy-done.6), kind=kOutput, calls=%fused_computation.38 | convolution fusion | flops 6442516480 | bytes 17039360 | tf_op jit(solution)/shard_map/cpkm,pmqj->cqkj/dot_general | solution.py:58
  277.9 9.3 %fusion.20 = f32[1024,2,8,128]{0,3,2,1:T(8,128)S(1)} fusion(f32[1024,2,8,128]{3,2,0,1:T(8,128)S(1)} %pad_maximum_fusion.1, f32[1,128,2,128]{1,3,0,2:T(8,128)S(1)} %get-tuple-element.39, f32[1,128,2,128]{1,3,0,2:T(8,128)S(1)} %copy-done.6), kind=kOutput, calls=%fused_computation.39 | convolution fusion | flops 6442516480 | bytes 17039360 | tf_op jit(solution)/shard_map/cpkm,pmqj->cqkj/dot_general | solution.py:58
  287.3 7.2 %pad_maximum_fusion.2 = f32[1024,2,8,128]{3,2,0,1:T(8,128)} fusion(f32[1024,1,8,128]{3,2,0,1:T(8,128)} %get-tuple-element.46, f32[1024,1,8,128]{3,2,0,1:T(8,128)} %get-tuple-element.47), kind=kLoop, calls=%fused_computation.2 | loop fusion | flops 2097152 | bytes 16777216 | tf_op jit(solution)/shard_map/stack | solution.py:51
  294.5 13.9 %fusion.23 = f32[1024,2,8,128]{0,3,2,1:T(8,128)S(1)} fusion(f32[1024,2,8,128]{3,2,0,1:T(8,128)} %pad_maximum_fusion.2, f32[1,128,2,128]{1,3,0,2:T(8,128)S(1)} %get-tuple-element.39, f32[1,128,2,128]{1,3,0,2:T(8,128)S(1)} %copy-done.6), kind=kOutput, calls=%fused_computation.40 | convolution fusion | flops 6442516480 | bytes 17039360 | tf_op jit(solution)/shard_map/cpkm,pmqj->cqkj/dot_general | solution.py:58
  308.4 4.3 multiply_add_fusion.1
  312.6 7.3 %subtract_subtract_fusion = (f32[1024,1,8,128]{0,3,2,1:T(8,128)}, f32[1024,1,8,128]{0,3,2,1:T(8,128)}) fusion(f32[1024,2,8,128]{0,3,2,1:T(8,128)} %fusion.17, f32[1024,2,8,128]{0,3,2,1:T(8,128)S(1)} %fusion.23, f32[1024,2,8,128]{0,3,2,1:T(8,128)S(1)} %fusion.20), kind=kLoop, calls=%fused_computation.31 | loop fusion | flops 14680064 | bytes 33554432 | tf_op jit(solution)/shard_map/sub | solution.py:91
  319.9 8.3 %maximum_bitcast_fusion = f32[1024,2,8,128,1]{0,3,2,1,4:T(8,128)} fusion(f32[1024,1,8,128]{0,3,2,1:T(8,128)} %get-tuple-element.21, f32[1024,1,8,128]{0,3,2,1:T(8,128)} %get-tuple-element.20), kind=kLoop, calls=%fused_computation.3 | loop fusion | flops 2097152 | bytes 16777216 | tf_op jit(solution)/shard_map/stack | solution.py:91
  328.3 9.2 %copy.149 = f32[1024,2,8,128,1]{3,2,1,0,4:T(8,128)} copy(f32[1024,2,8,128,1]{0,3,2,1,4:T(8,128)} %maximum_bitcast_fusion) | data formatting | bytes 16777216 | tf_op jit(solution)/shard_map/stack | solution.py:91
  337.5 8.3 %maximum_bitcast_fusion.1 = f32[1024,2,8,128,1]{0,3,2,1,4:T(8,128)} fusion(f32[1024,1,8,128]{0,3,2,1:T(8,128)} %get-tuple-element.23, f32[1024,1,8,128]{0,3,2,1:T(8,128)} %get-tuple-element.22), kind=kLoop, calls=%fused_computation.5 | loop fusion | flops 2097152 | bytes 16777216 | tf_op jit(solution)/shard_map/stack | solution.py:96
  345.9 9.3 %copy.154 = f32[1024,2,8,128,1]{3,2,1,0,4:T(8,128)} copy(f32[1024,2,8,128,1]{0,3,2,1,4:T(8,128)} %maximum_bitcast_fusion.1) | data formatting | bytes 16777216 | tf_op jit(solution)/shard_map/stack | solution.py:96
  355.2 10.2 %convolution_bitcast_fusion.1 = f32[1024,2,8,128]{3,2,0,1:T(8,128)S(1)} fusion(f32[1024,2,8,128,1]{3,2,1,0,4:T(8,128)} %copy.149, f32[1,128,2,128]{1,3,2,0:T(8,128)S(1)} %copy-done.9, f32[1,128,2,128]{1,3,2,0:T(8,128)S(1)} %copy-done.8), kind=kOutput, calls=%fused_computation.42 | convolution fusion | flops 6442516480 | bytes 17039360 | tf_op jit(solution)/shard_map/cpkm,pmqj->cqkj/dot_general | solution.py:63
  365.4 7.4 %convolution_bitcast_fusion = f32[1024,2,8,128]{3,2,0,1:T(8,128)S(1)} fusion(f32[1024,2,8,128,1]{3,2,1,0,4:T(8,128)S(1)} %copy-done.1, f32[1,128,2,128]{1,3,2,0:T(8,128)S(1)} %copy-done.9, f32[1,128,2,128]{1,3,2,0:T(8,128)S(1)} %copy-done.8), kind=kOutput, calls=%fused_computation.41 | convolution fusion | flops 6442516480 | bytes 17039360 | tf_op jit(solution)/shard_map/cpkm,pmqj->cqkj/dot_general | solution.py:63
  372.9 6.0 multiply_subtract_fusion
  378.8 11.9 %fusion.36 = bf16[1024,2,4,128]{3,2,0,1:T(4,128)(2,1)} fusion(f32[1,8,2,4]{1,3,0,2:T(4,128)S(1)} %copy-done.19, f32[1,8,2,4]{1,3,0,2:T(4,128)S(1)} %copy-done.18, f32[1024,1,8,128]{3,2,0,1:T(8,128)} %get-tuple-element.44, f32[1024,1,8,128]{3,2,0,1:T(8,128)} %get-tuple-element.45), kind=kOutput, calls=%fused_computation.63 | convolution fusion | flops 205521024 | bytes 10486272 | tf_op jit(solution)/shard_map/cpkm,pkqn->cqnm/dot_general | solution.py:73
  390.8 4.3 copy.167
  395.1 2.8 slice_bitcast_fusion
  400.2 7.8 %reduce.6 = bf16[512,1024]{1,0:T(8,128)(2,1)} reduce(bf16[512,1,1024]{2,1,0:T(2,128)(2,1)S(1)} %bitcast.267, bf16[]{:T(256)} %broadcast.196), dimensions={1}, to_apply=%bitcast.251.reduce_sub_computation | reduce | bytes 2097154
  408.0 3.7 reshape.280
  411.7 4.5 all-to-all-start.6
  417.9 6.8 %reduce.5 = bf16[512,1024]{1,0:T(8,128)(2,1)S(1)} reduce(bf16[512,1,1024]{2,1,0:T(2,128)(2,1)S(1)} %bitcast.268, bf16[]{:T(256)} %broadcast.196), dimensions={1}, to_apply=%bitcast.252.reduce_sub_computation | reduce | bytes 2097154
  426.7 14.8 %all-to-all-done.6 = bf16[4,2,65536]{2,1,0:T(2,128)(2,1)} async-done(((bf16[4,2,65536]{2,1,0:T(2,128)(2,1)}), bf16[4,2,65536]{2,1,0:T(2,128)(2,1)}, u32[]{:S(2)}, u32[]{:S(2)}) %all-to-all-start.6) | async-done | bytes 1048608 | tf_op jit(solution)/shard_map/all_to_all | solution.py:159
  441.5 3.5 all-to-all-start.5
  445.1 9.1 %fusion.30 = f32[1024,1,4,128]{3,2,0,1:T(4,128)} fusion(f32[1024,1,8,128]{3,2,0,1:T(8,128)} %get-tuple-element.25, f32[1024,1,8,128]{3,2,0,1:T(8,128)} %get-tuple-element.24, f32[1,8,1,4]{1,3,2,0:T(4,128)S(1)} %copy-done.16, f32[1,8,1,4]{1,3,2,0:T(4,128)S(1)} %copy-done.17), kind=kOutput, calls=%fused_computation.51 | convolution fusion | flops 103284800 | bytes 10486016 | tf_op jit(solution)/shard_map/cpkm,pkqn->cqnm/dot_general | solution.py:73
  454.2 3.1 copy.139
  460.7 7.8 %reduce.4 = bf16[512,1024]{1,0:T(8,128)(2,1)} reduce(bf16[512,1,1024]{2,1,0:T(2,128)(2,1)S(1)} %bitcast.262, bf16[]{:T(256)} %broadcast.196), dimensions={1}, to_apply=%bitcast.253.reduce_sub_computation | reduce | bytes 2097154
  468.4 4.0 reshape.276
  472.4 5.0 all-to-all-start.4
  477.5 32.8 %all-reduce.3.cloned.1.call-done = f32[1024,512]{0,1:T(8,128)} async-done(((f32[1024,512]{0,1:T(8,128)}), f32[1024,512]{0,1:T(8,128)}) %all-reduce.3.cloned.1.call-update) | async-done | bytes 2097168 | tf_op jit(solution)/shard_map/psum | solution.py:161
  510.2 4.8 fusion.48
  520.3 64.6 %all-reduce.5.cloned.1.call-done = f32[64,512]{1,0:T(8,128)} async-done(((f32[64,512]{1,0:T(8,128)}), f32[64,512]{1,0:T(8,128)}) %all-reduce.5.cloned.1.call-update) | async-done | bytes 131088 | tf_op jit(solution)/shard_map/psum | solution.py:165
  597.4 2.6 reshape.277
  (100 shorter events, 50.1 us)
Async XLA Ops:
  7.2 146.2 %copy-start = (f32[64,1024]{1,0:T(8,128)S(1)}, f32[64,1024]{1,0:T(8,128)}, u32[]{:S(2)}) copy-start(f32[64,1024]{1,0:T(8,128)} %param.12) | copy-start | bytes 786436
  36.9 38.2 %all-to-all-start = ((bf16[4,2,65536]{2,1,0:T(2,128)(2,1)}), bf16[4,2,65536]{2,1,0:T(2,128)(2,1)S(1)}, u32[]{:S(2)}, u32[]{:S(2)}) async-start(bf16[4,2,65536]{2,1,0:T(2,128)(2,1)} %reshape.268), calls=%async_computation | async-start | bytes 2097152 | tf_op jit(solution)/shard_map/all_to_all | solution.py:129
  75.2 1.0 copy-start.5
  76.1 71.9 %all-to-all-start.1 = ((bf16[4,2,65536]{2,1,0:T(2,128)(2,1)}), bf16[4,2,65536]{2,1,0:T(2,128)(2,1)S(1)}, u32[]{:S(2)}, u32[]{:S(2)}) async-start(bf16[4,2,65536]{2,1,0:T(2,128)(2,1)} %reshape.270), calls=%async_computation.1 | async-start | bytes 2097152 | tf_op jit(solution)/shard_map/all_to_all | solution.py:127
  113.6 32.2 %copy-start.20 = (f32[1024]{0:T(1024)S(1)}, f32[1024]{0:T(1024)}, u32[]{:S(2)}) copy-start(f32[1024]{0:T(1024)} %param.13) | copy-start | bytes 12292
  113.6 33.1 %copy-start.15 = (f32[32,64]{1,0:T(8,128)S(1)}, f32[32,64]{1,0:T(8,128)}, u32[]{:S(2)}) copy-start(f32[32,64]{1,0:T(8,128)} %param.11) | copy-start | bytes 24580
  145.9 12.9 %copy-start.21 = (f32[1024]{0:T(1024)}, f32[1024]{0:T(1024)S(1)}, u32[]{:S(2)}) copy-start(f32[1024]{0:T(1024)S(1)} %neg.33) | copy-start | bytes 12292
  146.1 0.6 copy-start.11
  146.1 0.6 copy-start.12
  148.0 8.7 %copy-start.13 = (f32[512,64]{0,1:T(8,128)}, f32[512,64]{0,1:T(8,128)S(1)}, u32[]{:S(2)}) copy-start(f32[512,64]{0,1:T(8,128)S(1)} %get-tuple-element.59) | copy-start | bytes 393220
  148.1 30.0 %all-to-all-start.2 = ((bf16[4,2,65536]{2,1,0:T(2,128)(2,1)}), bf16[4,2,65536]{2,1,0:T(2,128)(2,1)}, u32[]{:S(2)}, u32[]{:S(2)}) async-start(bf16[4,2,65536]{2,1,0:T(2,128)(2,1)} %reshape.272), calls=%async_computation.2 | async-start | bytes 2097152 | tf_op jit(solution)/shard_map/all_to_all | solution.py:128
  178.0 29.8 %all-to-all-start.3 = ((bf16[4,2,65536]{2,1,0:T(2,128)(2,1)}), bf16[4,2,65536]{2,1,0:T(2,128)(2,1)}, u32[]{:S(2)}, u32[]{:S(2)}) async-start(bf16[4,2,65536]{2,1,0:T(2,128)(2,1)} %reshape.274), calls=%async_computation.3 | async-start | bytes 2097152 | tf_op jit(solution)/shard_map/all_to_all | solution.py:126
  263.4 4.0 copy-start.6
  345.9 9.3 %copy-start.8 = (f32[1,128,2,128]{1,3,2,0:T(8,128)S(1)}, f32[1,128,2,128]{1,3,2,0:T(8,128)}, u32[]{:S(2)}) copy-start(f32[1,128,2,128]{1,3,2,0:T(8,128)} %get-tuple-element.38) | copy-start | bytes 393220
  345.9 9.3 %copy-start.9 = (f32[1,128,2,128]{1,3,2,0:T(8,128)S(1)}, f32[1,128,2,128]{1,3,2,0:T(8,128)}, u32[]{:S(2)}) copy-start(f32[1,128,2,128]{1,3,2,0:T(8,128)} %get-tuple-element.43) | copy-start | bytes 393220
  355.2 10.2 %copy-start.1 = (f32[1024,2,8,128,1]{3,2,1,0,4:T(8,128)S(1)}, f32[1024,2,8,128,1]{3,2,1,0,4:T(8,128)}, u32[]{:S(2)}) copy-start(f32[1024,2,8,128,1]{3,2,1,0,4:T(8,128)} %copy.154) | copy-start | bytes 25165828
  372.8 6.0 copy-start.18
  372.8 6.0 copy-start.19
  395.1 2.8 copy-start.2
  411.7 29.8 %all-to-all-start.6 = ((bf16[4,2,65536]{2,1,0:T(2,128)(2,1)}), bf16[4,2,65536]{2,1,0:T(2,128)(2,1)}, u32[]{:S(2)}, u32[]{:S(2)}) async-start(bf16[4,2,65536]{2,1,0:T(2,128)(2,1)} %reshape.280), calls=%async_computation.6 | async-start | bytes 2097152 | tf_op jit(solution)/shard_map/all_to_all | solution.py:159
  417.9 27.2 %copy-start.16 = (f32[1,8,1,4]{1,3,2,0:T(4,128)S(1)}, f32[1,8,1,4]{1,3,2,0:T(4,128)}, u32[]{:S(2)}) copy-start(f32[1,8,1,4]{1,3,2,0:T(4,128)} %get-tuple-element.52) | copy-start | bytes 388
  417.9 27.2 %copy-start.17 = (f32[1,8,1,4]{1,3,2,0:T(4,128)S(1)}, f32[1,8,1,4]{1,3,2,0:T(4,128)}, u32[]{:S(2)}) copy-start(f32[1,8,1,4]{1,3,2,0:T(4,128)} %get-tuple-element.68) | copy-start | bytes 388
  441.5 30.9 %all-to-all-start.5 = ((bf16[4,2,65536]{2,1,0:T(2,128)(2,1)}), bf16[4,2,65536]{2,1,0:T(2,128)(2,1)S(1)}, u32[]{:S(2)}, u32[]{:S(2)}) async-start(bf16[4,2,65536]{2,1,0:T(2,128)(2,1)} %reshape.278), calls=%async_computation.5 | async-start | bytes 2097152 | tf_op jit(solution)/shard_map/all_to_all | solution.py:158
  445.0 65.2 %all-reduce.3.cloned.1.call-start = ((), (), s32[]{:S(2)}) async-start(), calls=%async_computation.7 | async-start | bytes 4194304 | tf_op jit(solution)/shard_map/psum | solution.py:161
  454.2 3.1 copy-start.3
  460.6 49.6 %copy-start.22 = (f32[1024]{0:T(1024)S(1)}, f32[1024]{0:T(1024)}, u32[]{:S(2)}) copy-start(f32[1024]{0:T(1024)} %copy-done.21) | copy-start | bytes 12292
  468.4 46.6 %copy-start.4 = (f32[1024,512]{0,1:T(8,128)S(1)}, f32[1024,512]{0,1:T(8,128)}, u32[]{:S(2)}) copy-start(f32[1024,512]{0,1:T(8,128)} %bitcast_multiply_fusion.5) | copy-start | bytes 6291460
  472.4 124.9 %all-to-all-start.4 = ((bf16[4,2,65536]{2,1,0:T(2,128)(2,1)}), bf16[4,2,65536]{2,1,0:T(2,128)(2,1)}, u32[]{:S(2)}, u32[]{:S(2)}) async-start(bf16[4,2,65536]{2,1,0:T(2,128)(2,1)} %reshape.276), calls=%async_computation.4 | async-start | bytes 2097152 | tf_op jit(solution)/shard_map/all_to_all | solution.py:157
  477.4 107.5 %all-reduce.5.cloned.1.call-start = ((), (), s32[]{:S(2)}) async-start(), calls=%async_computation.8 | async-start | bytes 262144 | tf_op jit(solution)/shard_map/psum | solution.py:165
  515.0 69.9 %copy-start.10 = (f32[512,64]{0,1:T(8,128)S(1)}, f32[512,64]{0,1:T(8,128)}, u32[]{:S(2)}) copy-start(f32[512,64]{0,1:T(8,128)} %get-tuple-element.60) | copy-start | bytes 393220
  515.0 2.3 copy-start.7
  515.0 2.2 copy-start.14
Sparse Core Ops, SparseCore 0:
  457.4 52.7 all-reduce.2
  515.1 69.7 all-reduce.4
where the time goes:
time: 619 us; the launch traced here: 609 us
  other arithmetic  211 us (34%)
  local copies, waits for them, and re-layouts  122 us (20%)
  waiting for transfers between devices  118 us (19%)
  matrix products  109 us (18%)
  starting transfers between devices  34.7 us (6%)
  between operations  14.7 us (2%)
    unnamed x7, other arithmetic  115 us
    unnamed x71, local copies, waits for them, and re-layouts  68.4 us
    psum x1, waiting for transfers between devices, per_device(): hidden_grad = lax.psum(hidden_grad, ('chan', 'seq'))  64.6 us
    dot_general x3, matrix products, forward_spec(): jnp.einsum('cpkm,pmqj->cqkj', turned, last_forward, precision=lax.Precisi...  33.7 us
    psum x1, waiting for transfers between devices, per_device(): summed = lax.psum(correlation, 'dp')  32.8 us
    dot_general x3, matrix products, forward_spec(): jnp.einsum('cnm,nqk->cqkm', blocks, first_table, precision=lax.Precision....  22.6 us
    dot_general x2, matrix products, inverse_head(): jnp.einsum('cpkm,pkqn->cqnm', turned, middle, precision=lax.Precision.HIG...  21 us
    add x1, other arithmetic, forward_spec(): part_real * twist_cos + part_imag * twist_sin  17.7 us
  transfers between devices with their start and end apart: 9, of which 5 were waited for; matrix products, arithmetic and copies ran while one was open for 33% of the time, Pallas kernels for 0%

commit v1 on v0

v1 whole, which is shorter than its diff:
```python
import functools
import math

import jax
import jax.numpy as jnp
import numpy as np
from jax import lax
from jax.experimental import pallas as pl
from jax.experimental.pallas import tpu as pltpu
from jax.sharding import PartitionSpec as P

HIGHEST = lax.Precision.HIGHEST
MESH = pl.DeviceIdType.MESH
NARROW = jnp.bfloat16
WIDE = jnp.float32


def embed_features(length, count):
    bands = np.arange(count // 2) + 0.5
    phase = np.arange(length)[None, :] * bands[:, None] * (2.0 * np.pi / length)
    return np.concatenate([np.sin(phase), np.cos(phase)], axis=0).astype(np.float32)


def dft_tables(length):
    turns = np.outer(2 * np.arange(length) + 1, np.arange(length)) % (4 * length)
    angles = turns * (2.0 * np.pi / (4 * length))
    forward = np.concatenate([np.cos(angles), np.sin(angles)], axis=0)
    half = length // 2
    by_half = np.stack([forward[:, :half], forward[:, half:]])
    return by_half.astype(NARROW)


def dot(a, b, dims=((1,), (0,)), precision=None):
    return lax.dot_general(a, b, (dims, ((), ())), preferred_element_type=WIDE, precision=precision)


def doubling_steps(size):
    return [1 << i for i in range(size.bit_length() - 1)]


def flip(index, bit):
    return index + bit - 2 * bit * (lax.rem(lax.div(index, bit), 2))


def kernel(sizes, tile, q_ref, k_ref, v_ref, g_ref, hidden_ref, hidden_t_ref, cos_ref, feat_ref,
           filter_ref, rate_ref, fwd_ref, dq_ref, dk_ref, dv_ref, grad_ref, embed_ref,
           inv_ref, src, a_buf, b_buf, out_buf, ret_buf, hg_buf, g_sum, g_got, e_sum, e_got,
           in_send, in_recv, ret_send, ret_recv, red_send, red_recv, emb_send, emb_recv):
    n, dpn, chn = sizes
    half = n // 2
    rows, width = q_ref.shape
    length = rows * n
    span = rows * half
    group = width // half
    tiles = group // tile
    hid = hidden_t_ref.shape[0]
    me = lax.axis_index("seq")
    dp = lax.axis_index("dp")
    ch = lax.axis_index("chan")
    up = lax.div(me, half)
    slot = lax.rem(me, half)

    barrier = pltpu.get_barrier_semaphore()
    greeted = 0
    for o in range(1, n):
        pl.semaphore_signal(barrier, inc=1, device_id=(dp, ch, lax.rem(me + o, n)), device_id_type=MESH)
        greeted += 1
    for bit in doubling_steps(dpn):
        pl.semaphore_signal(barrier, inc=1, device_id=(flip(dp, bit), ch, me), device_id_type=MESH)
        greeted += 1
    for bit in doubling_steps(chn):
        pl.semaphore_signal(barrier, inc=1, device_id=(dp, flip(ch, bit), me), device_id_type=MESH)
        greeted += 1
    pl.semaphore_wait(barrier, greeted)

    def col(owner, t):
        return pl.ds(pl.multiple_of(owner * group + t * tile, 128), tile)

    def tcol(t):
        return pl.ds(pl.multiple_of(t * tile, 128), tile)

    my_rows = pl.ds(pl.multiple_of(slot * rows, 16), rows)

    def in_copy(t, o, kind):
        owner = lax.rem(slot + o, half)
        dest = (dp, ch, (up if kind < 2 else 1 - up) * half + owner)
        source = src.at[0 if kind == 0 else 1, :, col(owner, t)]
        if kind == 1:
            target = b_buf.at[my_rows, tcol(t)]
        else:
            target = a_buf.at[up, my_rows, tcol(t)]
        return pltpu.make_async_remote_copy(
            src_ref=source, dst_ref=target, send_sem=in_send.at[t, o, kind],
            recv_sem=in_recv.at[t, o, kind], device_id=dest, device_id_type=MESH)

    def in_kinds(o):
        return (0, 1, 2) if o else (2,)

    def ret_copy(t, o, j):
        owner = lax.rem(slot + o, half)
        return pltpu.make_async_remote_copy(
            src_ref=out_buf.at[j, pl.ds(pl.multiple_of(owner * rows, 16), rows), tcol(t)],
            dst_ref=ret_buf.at[j, :, col(slot, t)],
            send_sem=ret_send.at[t, o, j], recv_sem=ret_recv.at[t, o, j],
            device_id=(dp, ch, up * half + owner), device_id_type=MESH)

    @pl.loop(0, tiles)
    def _(t):
        for o in list(range(1, half)) + [0]:
            owner = lax.rem(slot + o, half)
            c = col(owner, t)
            p = k_ref[:, c].astype(WIDE) * v_ref[:, c].astype(WIDE)
            u = g_ref[:, c].astype(WIDE) * q_ref[:, c].astype(WIDE)
            src[1 - up, :, c] = p.astype(NARROW)
            src[up, :, c] = u.astype(NARROW)
            for kind in in_kinds(o):
                in_copy(t, o, kind).start()
        c = col(slot, t)
        a_buf[up, my_rows, tcol(t)] = src[0, :, c]
        b_buf[my_rows, tcol(t)] = src[1, :, c]

    sign = (2 * up - 1).astype(WIDE)
    scale = 1.0 / (length * math.sqrt(dpn * length))
    time_scale = 1.0 / math.sqrt(length)
    hg_buf[...] = jnp.zeros_like(hg_buf)
    for i in (0, 1):
        inv_ref[i] = fwd_ref[i].T

    @pl.loop(0, tiles)
    def _(t):
        tc = tcol(t)
        positions = lax.broadcasted_iota(jnp.int32, (length, tile), 0).astype(WIDE) * (1.0 / length)
        window = jnp.exp(-rate_ref[:, tc] * positions)
        wf = filter_ref[:, tc]
        taps = dot(hidden_ref[...], wf) * window
        taps_n = taps.astype(NARROW)
        h = dot(fwd_ref[0], taps_n[:span]) + dot(fwd_ref[1], taps_n[span:])
        hc, hs = h[:length] * (1.0 / length), h[length:] * (sign / length)
        for o in range(half):
            for kind in in_kinds(o):
                in_copy(t, o, kind).wait_recv()
        b = dot(fwd_ref[up], b_buf[:, tc])
        mine = dot(fwd_ref[up], a_buf[up, :, tc])
        other = dot(fwd_ref[1 - up], a_buf[1 - up, :, tc])
        a = mine + other
        ac, as_ = a[:length], a[length:]
        bc, bs = b[:length], b[length:]

        def join(x, y):
            return jnp.concatenate([x.astype(NARROW), y.astype(NARROW)], axis=0)

        out_buf[0, :, tc] = dot(inv_ref[up], join(hc * ac - hs * as_, hc * as_ + hs * ac)).astype(NARROW)
        out_buf[1, :, tc] = dot(inv_ref[up], join(hc * bc + hs * bs, hc * bs - hs * bc)).astype(NARROW)
        for o in range(1, half):
            for j in (0, 1):
                ret_copy(t, o, j).start()
        for j in (0, 1):
            ret_buf[j, :, col(slot, t)] = out_buf[j, my_rows, tc]
        m = mine + 0.5 * other
        mc, ms = m[:length], m[length:]
        corr_n = join(mc * bc + ms * bs, (mc * bs - ms * bc) * sign)
        corr = jnp.concatenate([dot(inv_ref[0], corr_n), dot(inv_ref[1], corr_n)], axis=0) * scale
        weighted = (corr * window).astype(NARROW)
        g_sum[0, 0:hid, tc] = dot(hidden_t_ref[...], weighted) * time_scale
        rate = -jnp.sum(positions * taps * corr, axis=0, keepdims=True) * time_scale
        g_sum[0, hid:hid + 8, tc] = jnp.broadcast_to(rate, (8, tile))
        hg_buf[...] += dot(weighted, wf, ((1,), (1,)))

    e_sum[0] = dot(feat_ref[...], hg_buf[...] * cos_ref[...], precision=HIGHEST) * time_scale

    def exchange_embed(i, dest):
        copy = pltpu.make_async_remote_copy(
            src_ref=e_sum.at[i], dst_ref=e_got.at[i], send_sem=emb_send.at[i],
            recv_sem=emb_recv.at[i], device_id=dest, device_id_type=MESH)
        copy.start()
        return copy

    i = 0
    for bit in doubling_steps(dpn):
        dest = (flip(dp, bit), ch, me)
        copy = pltpu.make_async_remote_copy(
            src_ref=g_sum.at[i], dst_ref=g_got.at[i], send_sem=red_send.at[i],
            recv_sem=red_recv.at[i], device_id=dest, device_id_type=MESH)
        copy.start()
        exchange_embed(i, dest).wait()
        e_sum[i + 1] = e_sum[i] + e_got[i]
        copy.wait()
        g_sum[i + 1] = g_sum[i] + g_got[i]
        i += 1
    grad_ref[...] = g_sum[i]
    dests = [(dp, flip(ch, bit), me) for bit in doubling_steps(chn)]
    dests += [(dp, ch, flip(me, bit)) for bit in doubling_steps(n)]
    for dest in dests:
        exchange_embed(i, dest).wait()
        e_sum[i + 1] = e_sum[i] + e_got[i]
        i += 1
    embed_ref[...] = e_sum[i]

    @pl.loop(0, tiles)
    def _(t):
        for o in range(half):
            if o:
                for j in (0, 1):
                    ret_copy(t, o, j).wait()
            for kind in in_kinds(o):
                in_copy(t, o, kind).wait_send()
            c = col(lax.rem(slot - o + half, half), t)
            conv_out = ret_buf[1 - up, :, c].astype(WIDE)
            conv_grad = ret_buf[up, :, c].astype(WIDE)
            dq_ref[:, c] = (g_ref[:, c].astype(WIDE) * conv_out).astype(NARROW)
            dk_ref[:, c] = (conv_grad * v_ref[:, c].astype(WIDE)).astype(NARROW)
            dv_ref[:, c] = (conv_grad * k_ref[:, c].astype(WIDE)).astype(NARROW)


def per_device(query_input, key_input, value_input, grad_output, w_embed, w_filter, decay_rates):
    n, dpn, chn = lax.axis_size("seq"), lax.axis_size("dp"), lax.axis_size("chan")
    rows, width = query_input.shape[1:]
    length = rows * n
    half = n // 2
    group = width // half
    tile = min(group, 512)
    tiles = group // tile
    emb, hid = w_embed.shape

    features = jnp.asarray(embed_features(length, emb))
    pre = dot(features, w_embed, ((0,), (0,)), HIGHEST)
    hidden = jnp.sin(pre)
    forward = dft_tables(length)

    straight = [(2 * s, s) for s in range(half)] + [(2 * s + 1, s + half) for s in range(half)]
    crossed = [(2 * s + 1, s) for s in range(half)] + [(2 * s, s + half) for s in range(half)]
    upper = lax.axis_index("seq") >= half
    joined = jnp.concatenate([w_filter, decay_rates[None, :]], axis=0)
    first = lax.ppermute(joined, "seq", straight)
    second = lax.ppermute(joined, "seq", crossed)
    params = jnp.where(
        upper, jnp.concatenate([second, first], axis=1), jnp.concatenate([first, second], axis=1))

    vmem = pl.BlockSpec(memory_space=pltpu.VMEM)
    dma = pltpu.SemaphoreType.DMA
    dp_steps = len(doubling_steps(dpn))
    steps = dp_steps + len(doubling_steps(chn)) + len(doubling_steps(n))
    block = jax.ShapeDtypeStruct((rows, width), NARROW)
    out = pl.pallas_call(
        functools.partial(kernel, (n, dpn, chn), tile),
        out_shape=(block, block, block, jax.ShapeDtypeStruct((hid + 8, group), WIDE),
                   jax.ShapeDtypeStruct((emb, hid), WIDE)),
        in_specs=[vmem] * 11,
        out_specs=(vmem,) * 5,
        scratch_shapes=[
            pltpu.VMEM((2, half * rows, 2 * length), NARROW),
            pltpu.VMEM((2, rows, width), NARROW),
            pltpu.VMEM((2, half * rows, group), NARROW),
            pltpu.VMEM((half * rows, group), NARROW),
            pltpu.VMEM((2, half * rows, group), NARROW),
            pltpu.VMEM((2, rows, width), NARROW),
            pltpu.VMEM((length, hid), WIDE),
            pltpu.VMEM((dp_steps + 1, hid + 8, group), WIDE),
            pltpu.VMEM((dp_steps, hid + 8, group), WIDE),
            pltpu.VMEM((steps + 1, emb, hid), WIDE),
            pltpu.VMEM((steps, emb, hid), WIDE),
            dma((tiles, half, 3)), dma((tiles, half, 3)),
            dma((tiles, half, 2)), dma((tiles, half, 2)),
            dma((dp_steps,)), dma((dp_steps,)),
            dma((steps,)), dma((steps,)),
        ],
        compiler_params=pltpu.CompilerParams(
            collective_id=0, has_side_effects=True, vmem_limit_bytes=60 * 1024 * 1024),
        cost_estimate=pl.CostEstimate(flops=10**10, bytes_accessed=10**7, transcendentals=10**6),
    )(query_input[0], key_input[0], value_input[0], grad_output[0],
      hidden.astype(NARROW), hidden.T.astype(NARROW), jnp.cos(pre), features,
      params[:hid].astype(NARROW), params[hid:], forward)
    d_query, d_key, d_value, partial, grad_embed = out

    mine = group // 2
    left, right = partial[:hid + 1, :mine], partial[:hid + 1, mine:]
    back_straight = [(b, a) for a, b in straight]
    back_crossed = [(b, a) for a, b in crossed]
    total = lax.ppermute(jnp.where(upper, right, left), "seq", back_straight)
    total = total + lax.ppermute(jnp.where(upper, left, right), "seq", back_crossed)
    return (d_query[None], d_key[None], d_value[None], total[:hid], total[hid], grad_embed)


def solution(mesh):
    block = P("dp", "seq", "chan")
    in_specs = (block, block, block, block, P(), P(None, ("chan", "seq")), P(("chan", "seq")))
    out_specs = (block, block, block, P(None, ("chan", "seq")), P(("chan", "seq")), P())
    return jax.shard_map(
        per_device, mesh=mesh, in_specs=in_specs, out_specs=out_specs, check_vma=False
    )
```

time: 619 us -> 130 us (0.21); the launches traced: 609 us -> 130 us
  other arithmetic: 211 us -> 2.29 us
  local copies, waits for them, and re-layouts: 122 us -> 9.06 us
  matrix products: 109 us -> 1.54 us
  waiting for transfers between devices: 118 us -> 13.5 us
  Pallas kernels: 0 us -> 93.2 us
  starting transfers between devices: 34.7 us -> 9.76 us
  between operations: 14.7 us -> 0.75 us
    unnamed x7 -> x0, other arithmetic: 115 us -> none
    dot_general x15 -> x1, matrix products: 109 us -> 1.54 us  [dot(): lax.dot_general(a, b, (dims, ((), ())), preferred_element_type=WIDE, prec...]
    psum x2 -> x0, waiting for transfers between devices: 97.4 us -> none  [the longest x1 64.6 us: per_device(): hidden_grad = lax.psum(hidden_grad, ('chan', 'seq'))]
    pallas_call x0 -> x1, Pallas kernels: none -> 93.2 us  [per_device(): pl.pallas_call(functools.partial(kernel, (n, dpn, chn), tile), out_shape=...]
    unnamed x71 -> x18, local copies, waits for them, and re-layouts: 68.4 us -> 4.81 us
    all_to_all x7 -> x0, starting transfers between devices: 34.6 us -> none  [the longest x1 6.32 us: per_device(): lax.all_to_all(grad_output, 'seq', split_axis=2, concat_axis=1, tiled=True)]
    another operation x8 -> x0, other arithmetic: 33.9 us -> none  [the longest x3 15.3 us: forward_spec(): jnp.stack([part_real * twist_cos + part_imag * twist_sin, part_imag * twi...]
    convert_element_type x7 -> x0, other arithmetic: 23.3 us -> none  [the longest x2 5.03 us: per_device(): d_query = (grad_all.astype(jnp.float32) * conv_wide).astype(jnp.bfloat16)]
  transfers between devices with their start and end apart: 9 -> 4, of which waited for: 5 -> 2; matrix products, arithmetic and copies ran while one was open for 33% -> 2% of each run, Pallas kernels for 0% -> 0%
where the time goes in v1:
time: 130 us
  Pallas kernels  93.2 us (72%)
  waiting for transfers between devices  13.5 us (10%)
  starting transfers between devices  9.76 us (8%)
  local copies, waits for them, and re-layouts  9.06 us (7%)
  other arithmetic  2.29 us (2%)
  matrix products  1.54 us (1%)
    pallas_call x1, Pallas kernels, per_device(): pl.pallas_call(functools.partial(kernel, (n, dpn, chn), tile), out_shape=...  93.2 us
    ppermute x1, waiting for transfers between devices, per_device(): lax.ppermute(jnp.where(upper, left, right), 'seq', back_crossed)  11 us
    unnamed x18, local copies, waits for them, and re-layouts  4.81 us
    ppermute x1, starting transfers between devices, per_device(): lax.ppermute(jnp.where(upper, left, right), 'seq', back_crossed)  4.32 us
    ppermute x1, starting transfers between devices, per_device(): second = lax.ppermute(joined, 'seq', crossed)  4.09 us
  transfers between devices with their start and end apart: 4, of which 2 were waited for; matrix products, arithmetic and copies ran while one was open for 2% of the time, Pallas kernels for 0%

profile of v1, /device:TPU:0, one launch (start us, length us, event | category | flops | bytes accessed | tf_op | source)
XLA Modules:
  0.0 130.0 jit_solution(9769003494976555146)
XLA Ops:
  0.6 0.0 copy-start
  0.6 0.0 copy-start.5
  0.7 1.0 pad_maximum_fusion
  1.7 4.1 %collective-permute-start = (f32[65,1024]{1,0:T(8,128)S(1)}, f32[65,1024]{1,0:T(8,128)S(1)}, u32[]{:S(2)}, u32[]{:S(2)}) collective-permute-start(f32[65,1024]{1,0:T(8,128)S(1)} %pad_maximum_fusion), channel_id=1, source_target_pairs={{1,0},{3,1},{0,2},{2,3},{5,4},{7,5},{4,6},{6,7},{9,8},{11,9},{8,10... | collective-permute-start | bytes 798728 | tf_op jit(solution)/shard_map/ppermute | solution.py:235
  5.8 0.7 collective-permute-start.1
  6.5 0.0 copy-done
  6.5 0.0 copy-done.5
  6.5 1.5 %fusion = (f32[512,64]{0,1:T(8,128)S(1)}, bf16[512,64]{0,1:T(8,128)(2,1)S(1)}) fusion(f32[32,512]{1,0:T(8,128)S(1)} %copy-done.5, f32[32,64]{1,0:T(8,128)S(1)} %copy-done), kind=kOutput, calls=%fused_computation.6 | convolution fusion | flops 12615680 | bytes 270336 | tf_op jit(solution)/shard_map/dot_general | solution.py:34
  8.0 0.0 copy-start.4
  8.0 0.8 copy.17.hidden_ref
  8.8 0.0 copy-done.4
  8.8 0.8 copy.18.cos_ref
  9.6 2.5 %collective-permute-done = f32[65,1024]{1,0:T(8,128)S(1)} collective-permute-done((f32[65,1024]{1,0:T(8,128)S(1)}, f32[65,1024]{1,0:T(8,128)S(1)}, u32[]{:S(2)}, u32[]{:S(2)}) %collective-permute-start) | collective-permute-done | bytes 266272 | tf_op jit(solution)/shard_map/ppermute | solution.py:235
  12.1 0.0 collective-permute-done.1
  12.1 0.1 maximum_select_fusion
  12.1 0.7 slice.34.filter_ref
  12.9 0.6 slice.26.rate_ref
  13.5 93.2 %shard_map.136 = (bf16[128,4096]{1,0:T(8,128)(2,1)}, bf16[128,4096]{1,0:T(8,128)(2,1)}, bf16[128,4096]{1,0:T(8,128)(2,1)}, f32[72,2048]{1,0:T(8,128)}, f32[32,64]{1,0:T(8,128)}) custom-call(bf16[128,4096]{1,0:T(8,128)(2,1)} %bitcast.18, bf16[128,4096]{1,0:T(8,128)(2,1)} %bitcast.19, bf16[128,4096]{1,0:T(8,128)(2,1)} %bitcast.20, bf16[128,4096]{1,0:T(8,128)(2,1)} %bitcast.21, ...), custom_call_target="tpu_custom_call" | custom-call | flops 10000000000 | bytes 10000000 | tf_op jit(solution)/shard_map/pallas_call | solution.py:244
  106.6 0.0 copy-start.3
  106.7 1.2 slice_select_fusion
  107.8 0.7 collective-permute-start.2
  108.5 4.3 %collective-permute-start.3 = (f32[65,1024]{1,0:T(8,128)S(1)}, f32[65,1024]{1,0:T(8,128)S(1)}, u32[]{:S(2)}, u32[]{:S(2)}) collective-permute-start(f32[65,1024]{1,0:T(8,128)S(1)} %get-tuple-element.16), channel_id=1, source_target_pairs={{0,1},{1,3},{2,0},{3,2},{4,5},{5,7},{6,4},{7,6},{8,9},{9,11},{10,8... | collective-permute-start | bytes 798728 | tf_op jit(solution)/shard_map/ppermute | solution.py:280
  112.9 0.0 collective-permute-done.2
  112.9 11.0 %collective-permute-done.3 = f32[65,1024]{1,0:T(8,128)S(1)} collective-permute-done((f32[65,1024]{1,0:T(8,128)S(1)}, f32[65,1024]{1,0:T(8,128)S(1)}, u32[]{:S(2)}, u32[]{:S(2)}) %collective-permute-start.3) | collective-permute-done | bytes 266272 | tf_op jit(solution)/shard_map/ppermute | solution.py:280
  123.9 0.7 slice.27
  124.6 0.6 slice.28
  125.2 0.0 copy-done.3
  125.2 0.0 copy-start.2
  125.2 1.0 copy.23
  126.2 0.6 copy-done.2
  126.8 0.0 copy-start.1
  126.8 1.0 copy.24
  127.8 0.6 copy-done.1
  128.5 0.0 copy-start.6
  128.5 1.0 copy.25
  129.4 0.0 copy-done.6
  129.4 0.6 copy.26
  (1 shorter events, 0.0 us)
Async XLA Ops:
  0.6 5.8 %copy-start = (f32[32,64]{1,0:T(8,128)S(1)}, f32[32,64]{1,0:T(8,128)}, u32[]{:S(2)}) copy-start(f32[32,64]{1,0:T(8,128)} %param.13) | copy-start | bytes 24580
  0.6 5.8 %copy-start.5 = (f32[32,512]{1,0:T(8,128)S(1)}, f32[32,512]{1,0:T(8,128)}, u32[]{:S(2)}) copy-start(f32[32,512]{1,0:T(8,128)} %constant.10.clone.feat_ref) | copy-start | bytes 196612
  1.7 10.4 %collective-permute-start = (f32[65,1024]{1,0:T(8,128)S(1)}, f32[65,1024]{1,0:T(8,128)S(1)}, u32[]{:S(2)}, u32[]{:S(2)}) collective-permute-start(f32[65,1024]{1,0:T(8,128)S(1)} %pad_maximum_fusion), channel_id=1, source_target_pairs={{1,0},{3,1},{0,2},{2,3},{5,4},{7,5},{4,6},{6,7},{9,8},{11,9},{8,10... | collective-permute-start | bytes 798728 | tf_op jit(solution)/shard_map/ppermute | solution.py:235
  5.8 6.3 %collective-permute-start.1 = (f32[65,1024]{1,0:T(8,128)S(1)}, f32[65,1024]{1,0:T(8,128)S(1)}, u32[]{:S(2)}, u32[]{:S(2)}) collective-permute-start(f32[65,1024]{1,0:T(8,128)S(1)} %pad_maximum_fusion), channel_id=1, source_target_pairs={{0,0},{2,1},{1,2},{3,3},{4,4},{6,5},{5,6},{7,7},{8,8},{10,9},{9,10... | collective-permute-start | bytes 798728 | tf_op jit(solution)/shard_map/ppermute | solution.py:234
  8.0 0.8 copy-start.4
  106.6 18.6 %copy-start.3 = (bf16[128,4096]{1,0:T(8,128)(2,1)S(1)}, bf16[128,4096]{1,0:T(8,128)(2,1)}, u32[]{:S(2)}) copy-start(bf16[128,4096]{1,0:T(8,128)(2,1)} %get-tuple-element.11) | copy-start | bytes 3145732
  107.8 5.0 %collective-permute-start.2 = (f32[65,1024]{1,0:T(8,128)S(1)}, f32[65,1024]{1,0:T(8,128)S(1)}, u32[]{:S(2)}, u32[]{:S(2)}) collective-permute-start(f32[65,1024]{1,0:T(8,128)S(1)} %get-tuple-element.17), channel_id=1, source_target_pairs={{0,0},{1,2},{2,1},{3,3},{4,4},{5,6},{6,5},{7,7},{8,8},{9,10},{10,9... | collective-permute-start | bytes 798728 | tf_op jit(solution)/shard_map/ppermute | solution.py:279
  108.5 15.4 %collective-permute-start.3 = (f32[65,1024]{1,0:T(8,128)S(1)}, f32[65,1024]{1,0:T(8,128)S(1)}, u32[]{:S(2)}, u32[]{:S(2)}) collective-permute-start(f32[65,1024]{1,0:T(8,128)S(1)} %get-tuple-element.16), channel_id=1, source_target_pairs={{0,1},{1,3},{2,0},{3,2},{4,5},{5,7},{6,4},{7,6},{8,9},{9,11},{10,8... | collective-permute-start | bytes 798728 | tf_op jit(solution)/shard_map/ppermute | solution.py:280
  125.2 1.6 %copy-start.2 = (bf16[128,4096]{1,0:T(8,128)(2,1)S(1)}, bf16[128,4096]{1,0:T(8,128)(2,1)}, u32[]{:S(2)}) copy-start(bf16[128,4096]{1,0:T(8,128)(2,1)} %get-tuple-element.12) | copy-start | bytes 3145732
  126.8 1.6 %copy-start.1 = (bf16[128,4096]{1,0:T(8,128)(2,1)S(1)}, bf16[128,4096]{1,0:T(8,128)(2,1)}, u32[]{:S(2)}) copy-start(bf16[128,4096]{1,0:T(8,128)(2,1)} %get-tuple-element.13) | copy-start | bytes 3145732
  128.5 1.0 copy-start.6

commit v2 on v1

v2 whole, which is shorter than its diff:
```python
import functools
import math

import jax
import jax.numpy as jnp
import numpy as np
from jax import lax
from jax.experimental import pallas as pl
from jax.experimental.pallas import tpu as pltpu
from jax.sharding import PartitionSpec as P

HIGHEST = lax.Precision.HIGHEST
MESH = pl.DeviceIdType.MESH
NARROW = jnp.bfloat16
WIDE = jnp.float32


def embed_features(length, count):
    bands = np.arange(count // 2) + 0.5
    phase = np.arange(length)[None, :] * bands[:, None] * (2.0 * np.pi / length)
    return np.concatenate([np.sin(phase), np.cos(phase)], axis=0).astype(np.float32)


def dft_tables(length):
    turns = np.outer(2 * np.arange(length) + 1, np.arange(length)) % (4 * length)
    angles = turns * (2.0 * np.pi / (4 * length))
    forward = np.concatenate([np.cos(angles), np.sin(angles)], axis=0)
    half = length // 2
    by_half = np.stack([forward[:, :half], forward[:, half:]])
    return by_half.astype(NARROW)


def dot(a, b, dims=((1,), (0,)), precision=None):
    return lax.dot_general(a, b, (dims, ((), ())), preferred_element_type=WIDE, precision=precision)


def doubling_steps(size):
    return [1 << i for i in range(size.bit_length() - 1)]


def flip(index, bit):
    return index + bit - 2 * bit * (lax.rem(lax.div(index, bit), 2))


def kernel(sizes, tile, q_ref, k_ref, v_ref, g_ref, hidden_ref, hidden_t_ref, cos_ref, feat_ref,
           filter_ref, rate_ref, fwd_ref, conv_ref, grad_ref, embed_ref,
           inv_ref, src, a_buf, b_buf, out_buf, h_buf, taps_buf, win_buf, taps_n, corr_buf, weighted_n,
           mine_buf, other_buf, b_spec, join_1, join_2, join_3,
           filter_buf, rate_buf, hg_buf, g_sum, g_got, fin_src, fin_got, e_sum, e_got,
           in_send, in_recv, ret_send, ret_recv, own_sem, red_send, red_recv, emb_send, emb_recv,
           par_send, par_recv, rat_send, rat_recv, fin_send, fin_recv):
    n, dpn, chn = sizes
    half = n // 2
    rows, width = q_ref.shape
    length = rows * n
    span = rows * half
    group = width // half
    part = group // 2
    tiles = group // tile
    hid = hidden_t_ref.shape[0]
    me = lax.axis_index("seq")
    dp = lax.axis_index("dp")
    ch = lax.axis_index("chan")
    up = lax.div(me, half)
    slot = lax.rem(me, half)
    pair = lax.div(me, 2)
    parity = lax.rem(me, 2)

    barrier = pltpu.get_barrier_semaphore()
    greeted = 0
    for o in range(1, n):
        pl.semaphore_signal(barrier, inc=1, device_id=(dp, ch, lax.rem(me + o, n)), device_id_type=MESH)
        greeted += 1
    for bit in doubling_steps(dpn):
        pl.semaphore_signal(barrier, inc=1, device_id=(flip(dp, bit), ch, me), device_id_type=MESH)
        greeted += 1
    for bit in doubling_steps(chn):
        pl.semaphore_signal(barrier, inc=1, device_id=(dp, flip(ch, bit), me), device_id_type=MESH)
        greeted += 1
    pl.semaphore_wait(barrier, greeted)

    def col(owner, t):
        return pl.ds(pl.multiple_of(owner * group + t * tile, 128), tile)

    def tcol(t):
        return pl.ds(pl.multiple_of(t * tile, 128), tile)

    def block_rows(i, size, base=0):
        return pl.ds(pl.multiple_of(base + i * size, 16), size)

    my_rows = pl.ds(pl.multiple_of(slot * rows, 16), rows)

    def par_copies(j):
        dest = (dp, ch, pair + j * half)
        return [
            pltpu.make_async_remote_copy(
                src_ref=source, dst_ref=target.at[parity], send_sem=send.at[j],
                recv_sem=recv.at[parity], device_id=dest, device_id_type=MESH)
            for source, target, send, recv in (
                (filter_ref, filter_buf, par_send, par_recv), (rate_ref, rate_buf, rat_send, rat_recv))]

    def par_arrivals(e):
        return [
            pltpu.make_async_remote_copy(
                src_ref=source, dst_ref=target.at[e], send_sem=send.at[0],
                recv_sem=recv.at[e], device_id=(dp, ch, lax.rem(me + 1, n)), device_id_type=MESH)
            for source, target, send, recv in (
                (filter_ref, filter_buf, par_send, par_recv), (rate_ref, rate_buf, rat_send, rat_recv))]

    for j in (0, 1):
        @pl.when(pair + j * half != me)
        def _():
            for copy in par_copies(j):
                copy.start()

        @pl.when(pair + j * half == me)
        def _():
            filter_buf[parity] = filter_ref[...]
            rate_buf[parity] = rate_ref[...]

    def in_copy(t, o, kind):
        owner = lax.rem(slot + o, half)
        dest = (dp, ch, (up if kind < 2 else 1 - up) * half + owner)
        source = src.at[0 if kind == 0 else 1, :, col(owner, t)]
        if kind == 1:
            target = b_buf.at[my_rows, tcol(t)]
        else:
            target = a_buf.at[up, my_rows, tcol(t)]
        return pltpu.make_async_remote_copy(
            src_ref=source, dst_ref=target, send_sem=in_send.at[t, o, kind],
            recv_sem=in_recv.at[t, o, kind], device_id=dest, device_id_type=MESH)

    def in_kinds(o):
        return (0, 1, 2) if o else (2,)

    def ret_target(t, j):
        return conv_ref.at[1 - up if j == 0 else up, :, col(slot, t)]

    def ret_copy(t, o, j):
        owner = lax.rem(slot + o, half)
        return pltpu.make_async_remote_copy(
            src_ref=out_buf.at[j, pl.ds(pl.multiple_of(owner * rows, 16), rows), tcol(t)],
            dst_ref=ret_target(t, j),
            send_sem=ret_send.at[t, o, j], recv_sem=ret_recv.at[t, o, j],
            device_id=(dp, ch, up * half + owner), device_id_type=MESH)

    def own_copy(t, j):
        return pltpu.make_async_copy(out_buf.at[j, my_rows, tcol(t)], ret_target(t, j), own_sem.at[t, j])

    @pl.loop(0, tiles)
    def _(t):
        for o in list(range(1, half)) + [0]:
            owner = lax.rem(slot + o, half)
            c = col(owner, t)
            p = k_ref[:, c].astype(WIDE) * v_ref[:, c].astype(WIDE)
            u = g_ref[:, c].astype(WIDE) * q_ref[:, c].astype(WIDE)
            src[1 - up, :, c] = p.astype(NARROW)
            src[up, :, c] = u.astype(NARROW)
            for kind in in_kinds(o):
                in_copy(t, o, kind).start()
        c = col(slot, t)
        a_buf[up, my_rows, tcol(t)] = src[0, :, c]
        b_buf[my_rows, tcol(t)] = src[1, :, c]

    sign = (2 * up - 1).astype(WIDE)
    scale = 1.0 / (length * math.sqrt(dpn * length))
    time_scale = 1.0 / math.sqrt(length)
    hg_buf[...] = jnp.zeros_like(hg_buf)
    for i in (0, 1):
        inv_ref[i] = fwd_ref[i].T
    for e in (0, 1):
        @pl.when(2 * slot + e != me)
        def _():
            for copy in par_arrivals(e):
                copy.wait_recv()

    def pick(ref, t):
        if tile <= part:
            per = part // tile
            return ref[lax.div(t, per), :, tcol(lax.rem(t, per))]
        return jnp.concatenate([ref[0], ref[1]], axis=1)

    step = 32

    def places(i):
        at = lax.broadcasted_iota(jnp.int32, (step, tile), 0) + i * step
        return at.astype(WIDE) * (1.0 / length)

    @pl.loop(0, tiles)
    def _(t):
        tc = tcol(t)
        corr_buf[...] = dot(hidden_ref[...], pick(filter_buf, t))
        rate = pick(rate_buf, t)[0:1]

        @pl.loop(0, length // step)
        def _(i):
            r = block_rows(i, step)
            window = jnp.exp(-rate * places(i))
            taps = corr_buf[r, :] * window
            win_buf[r, tc] = window
            taps_buf[r, tc] = taps
            taps_n[r, :] = (taps * (1.0 / length)).astype(NARROW)

        h_buf[:, tc] = dot(fwd_ref[0], taps_n[:span]) + dot(fwd_ref[1], taps_n[span:])

    @pl.loop(0, tiles)
    def _(t):
        tc = tcol(t)
        for o in range(half):
            for kind in in_kinds(o):
                in_copy(t, o, kind).wait_recv()
        b_spec[...] = dot(fwd_ref[up], b_buf[:, tc])
        mine_buf[...] = dot(fwd_ref[up], a_buf[up, :, tc])
        other_buf[...] = dot(fwd_ref[1 - up], a_buf[1 - up, :, tc])

        @pl.loop(0, length // step)
        def _(i):
            c, s = block_rows(i, step), block_rows(i, step, length)
            hc, hs = h_buf[c, tc], h_buf[s, tc] * sign
            bc, bs = b_spec[c, :], b_spec[s, :]
            mc, ms = mine_buf[c, :], mine_buf[s, :]
            oc, os = other_buf[c, :], other_buf[s, :]
            ac, as_ = mc + oc, ms + os
            join_1[c, :] = (hc * ac - hs * as_).astype(NARROW)
            join_1[s, :] = (hc * as_ + hs * ac).astype(NARROW)
            join_2[c, :] = (hc * bc + hs * bs).astype(NARROW)
            join_2[s, :] = (hc * bs - hs * bc).astype(NARROW)
            mc, ms = mc + 0.5 * oc, ms + 0.5 * os
            join_3[c, :] = (mc * bc + ms * bs).astype(NARROW)
            join_3[s, :] = ((mc * bs - ms * bc) * sign).astype(NARROW)

        out_buf[0, :, tc] = dot(inv_ref[up], join_1[...]).astype(NARROW)
        out_buf[1, :, tc] = dot(inv_ref[up], join_2[...]).astype(NARROW)
        for o in range(1, half):
            for j in (0, 1):
                ret_copy(t, o, j).start()
        for j in (0, 1):
            own_copy(t, j).start()
        for i in (0, 1):
            corr_buf[i * span:(i + 1) * span] = dot(inv_ref[i], join_3[...])

        def finish(i, rate):
            r = block_rows(i, step)
            corr = corr_buf[r, :] * scale
            weighted_n[r, :] = (corr * win_buf[r, tc]).astype(NARROW)
            return rate + jnp.sum(places(i) * taps_buf[r, tc] * corr, axis=0, keepdims=True)

        rate = lax.fori_loop(0, length // step, finish, jnp.zeros((1, tile), WIDE))
        g_sum[0, 0:hid, tc] = dot(hidden_t_ref[...], weighted_n[...]) * time_scale
        g_sum[0, hid:hid + 8, tc] = jnp.broadcast_to(rate * -time_scale, (8, tile))
        hg_buf[...] += dot(weighted_n[...], pick(filter_buf, t), ((1,), (1,)))

    def exchange_embed(i, dest):
        copy = pltpu.make_async_remote_copy(
            src_ref=e_sum.at[i], dst_ref=e_got.at[i], send_sem=emb_send.at[i],
            recv_sem=emb_recv.at[i], device_id=dest, device_id_type=MESH)
        copy.start()
        return copy

    i = 0
    for bit in doubling_steps(dpn):
        dest = (flip(dp, bit), ch, me)
        copy = pltpu.make_async_remote_copy(
            src_ref=g_sum.at[i], dst_ref=g_got.at[i], send_sem=red_send.at[i],
            recv_sem=red_recv.at[i], device_id=dest, device_id_type=MESH)
        copy.start()
        if i == 0:
            e_sum[0] = dot(feat_ref[...], hg_buf[...] * cos_ref[...], precision=HIGHEST) * time_scale
        exchange_embed(i, dest).wait()
        e_sum[i + 1] = e_sum[i] + e_got[i]
        copy.wait()
        g_sum[i + 1] = g_sum[i] + g_got[i]
        i += 1

    for e in (0, 1):
        fin_src[e] = g_sum[i, :, e * part:(e + 1) * part]

    def fin_copy(e):
        return pltpu.make_async_remote_copy(
            src_ref=fin_src.at[e], dst_ref=fin_got.at[up], send_sem=fin_send.at[e],
            recv_sem=fin_recv.at[up], device_id=(dp, ch, 2 * slot + e), device_id_type=MESH)

    def fin_arrival(j):
        return pltpu.make_async_remote_copy(
            src_ref=fin_src.at[0], dst_ref=fin_got.at[j], send_sem=fin_send.at[0],
            recv_sem=fin_recv.at[j], device_id=(dp, ch, lax.rem(me + 1, n)), device_id_type=MESH)

    for e in (0, 1):
        @pl.when(2 * slot + e != me)
        def _():
            fin_copy(e).start()

        @pl.when(2 * slot + e == me)
        def _():
            fin_got[up] = fin_src[e]

    dests = [(dp, flip(ch, bit), me) for bit in doubling_steps(chn)]
    dests += [(dp, ch, flip(me, bit)) for bit in doubling_steps(n)]
    for dest in dests:
        exchange_embed(i, dest).wait()
        e_sum[i + 1] = e_sum[i] + e_got[i]
        i += 1
    embed_ref[...] = e_sum[i]

    for j in (0, 1):
        @pl.when(pair + j * half != me)
        def _():
            fin_arrival(j).wait_recv()
            for copy in par_copies(j):
                copy.wait_send()
    for e in (0, 1):
        @pl.when(2 * slot + e != me)
        def _():
            fin_copy(e).wait_send()
    grad_ref[...] = fin_got[0] + fin_got[1]

    @pl.loop(0, tiles)
    def _(t):
        for o in range(half):
            for j in (0, 1):
                if o:
                    ret_copy(t, o, j).wait()
                else:
                    own_copy(t, j).wait()
            for kind in in_kinds(o):
                in_copy(t, o, kind).wait_send()


def per_device(query_input, key_input, value_input, grad_output, w_embed, w_filter, decay_rates):
    n, dpn, chn = lax.axis_size("seq"), lax.axis_size("dp"), lax.axis_size("chan")
    rows, width = query_input.shape[1:]
    length = rows * n
    half = n // 2
    span = half * rows
    group = width // half
    part = group // 2
    tile = min(group, 256)
    tiles = group // tile
    emb, hid = w_embed.shape

    features = jnp.asarray(embed_features(length, emb))
    pre = dot(features, w_embed, ((0,), (0,)), HIGHEST)
    hidden = jnp.sin(pre)
    forward = dft_tables(length)

    vmem = pl.BlockSpec(memory_space=pltpu.VMEM)
    dma = pltpu.SemaphoreType.DMA
    dp_steps = len(doubling_steps(dpn))
    steps = dp_steps + len(doubling_steps(chn)) + len(doubling_steps(n))
    conv, partial, grad_embed = pl.pallas_call(
        functools.partial(kernel, (n, dpn, chn), tile),
        out_shape=(jax.ShapeDtypeStruct((2, rows, width), NARROW),
                   jax.ShapeDtypeStruct((hid + 8, part), WIDE),
                   jax.ShapeDtypeStruct((emb, hid), WIDE)),
        in_specs=[vmem] * 11,
        out_specs=(pl.BlockSpec(memory_space=pl.ANY), vmem, vmem),
        scratch_shapes=[
            pltpu.VMEM((2, span, 2 * length), NARROW),
            pltpu.VMEM((2, rows, width), NARROW),
            pltpu.VMEM((2, span, group), NARROW),
            pltpu.VMEM((span, group), NARROW),
            pltpu.VMEM((2, span, group), NARROW),
            pltpu.VMEM((2 * length, group), WIDE),
            pltpu.VMEM((length, group), WIDE),
            pltpu.VMEM((length, group), WIDE),
            pltpu.VMEM((length, tile), NARROW),
            pltpu.VMEM((length, tile), WIDE),
            pltpu.VMEM((length, tile), NARROW),
            pltpu.VMEM((2 * length, tile), WIDE),
            pltpu.VMEM((2 * length, tile), WIDE),
            pltpu.VMEM((2 * length, tile), WIDE),
            pltpu.VMEM((2 * length, tile), NARROW),
            pltpu.VMEM((2 * length, tile), NARROW),
            pltpu.VMEM((2 * length, tile), NARROW),
            pltpu.VMEM((2, hid, part), NARROW),
            pltpu.VMEM((2, 8, part), WIDE),
            pltpu.VMEM((length, hid), WIDE),
            pltpu.VMEM((dp_steps + 1, hid + 8, group), WIDE),
            pltpu.VMEM((dp_steps, hid + 8, group), WIDE),
            pltpu.VMEM((2, hid + 8, part), WIDE),
            pltpu.VMEM((2, hid + 8, part), WIDE),
            pltpu.VMEM((steps + 1, emb, hid), WIDE),
            pltpu.VMEM((steps, emb, hid), WIDE),
            dma((tiles, half, 3)), dma((tiles, half, 3)),
            dma((tiles, half, 2)), dma((tiles, half, 2)), dma((tiles, 2)),
            dma((dp_steps,)), dma((dp_steps,)),
            dma((steps,)), dma((steps,)),
            dma((2,)), dma((2,)), dma((2,)), dma((2,)), dma((2,)), dma((2,)),
        ],
        compiler_params=pltpu.CompilerParams(
            collective_id=0, has_side_effects=True, vmem_limit_bytes=60 * 1024 * 1024),
        cost_estimate=pl.CostEstimate(flops=10**10, bytes_accessed=10**7, transcendentals=10**6),
    )(query_input[0], key_input[0], value_input[0], grad_output[0],
      hidden.astype(NARROW), hidden.T.astype(NARROW), jnp.cos(pre), features,
      w_filter.astype(NARROW), jnp.broadcast_to(decay_rates[None, :], (8, part)), forward)

    conv_out, conv_grad = conv[0:1].astype(WIDE), conv[1:2].astype(WIDE)
    d_query = (grad_output.astype(WIDE) * conv_out).astype(NARROW)
    d_key = (conv_grad * value_input.astype(WIDE)).astype(NARROW)
    d_value = (conv_grad * key_input.astype(WIDE)).astype(NARROW)
    return (d_query, d_key, d_value, partial[:hid], partial[hid], grad_embed)


def solution(mesh):
    block = P("dp", "seq", "chan")
    in_specs = (block, block, block, block, P(), P(None, ("chan", "seq")), P(("chan", "seq")))
    out_specs = (block, block, block, P(None, ("chan", "seq")), P(("chan", "seq")), P())
    return jax.shard_map(
        per_device, mesh=mesh, in_specs=in_specs, out_specs=out_specs, check_vma=False
    )
```

time: 130 us -> 114 us (0.88)
  waiting for transfers between devices: 13.5 us -> 0 us
  starting transfers between devices: 9.76 us -> 0 us
  Pallas kernels: 93.2 us -> 98.8 us
  other arithmetic: 2.29 us -> 5.62 us
  local copies, waits for them, and re-layouts: 9.06 us -> 6.57 us
    ppermute x4 -> x0, waiting for transfers between devices: 13.5 us -> none  [the longest x1 11 us: per_device(): lax.ppermute(jnp.where(upper, left, right), 'seq', back_crossed)]
    ppermute x4 -> x0, starting transfers between devices: 9.76 us -> none  [the longest x1 4.32 us: per_device(): lax.ppermute(jnp.where(upper, left, right), 'seq', back_crossed)]
    convert_element_type x0 -> x2, other arithmetic: none -> 5.62 us  [the longest x1 4 us: per_device(): d_value = (conv_grad * key_input.astype(WIDE)).astype(NARROW)]
    pallas_call x1, Pallas kernels: 93.2 us -> 98.8 us  [per_device(): pl.pallas_call(functools.partial(kernel, (n, dpn, chn), tile), out_shape=...]
    unnamed x18 -> x13, local copies, waits for them, and re-layouts: 4.81 us -> 0.64 us
    broadcast_in_dim x0 -> x1, local copies, waits for them, and re-layouts: none -> 1.31 us  [per_device(): jnp.broadcast_to(decay_rates[None, :], (8, part))]
    slice x4 -> x2, local copies, waits for them, and re-layouts: 2.65 us -> 3.02 us  [per_device(): return (d_query, d_key, d_value, partial[:hid], partial[hid], grad_embed)]
  transfers between devices with their start and end apart: 4 -> 0, of which waited for: 2 -> 0; matrix products, arithmetic and copies ran while one was open for 2% -> 0% of each run, Pallas kernels for 0% -> 0%
where the time goes in v2:
time: 114 us; the launch traced here: 113 us
  Pallas kernels  98.8 us (87%)
  local copies, waits for them, and re-layouts  6.57 us (6%)
  other arithmetic  5.62 us (5%)
  matrix products  1.6 us (1%)
    pallas_call x1, Pallas kernels, per_device(): pl.pallas_call(functools.partial(kernel, (n, dpn, chn), tile), out_shape=...  98.8 us
    convert_element_type x1, other arithmetic, per_device(): d_value = (conv_grad * key_input.astype(WIDE)).astype(NARROW)  4 us
    slice x2, local copies, waits for them, and re-layouts, per_device(): return (d_query, d_key, d_value, partial[:hid], partial[hid], grad_embed)  3.02 us

profile of v2, /device:TPU:0, one launch (start us, length us, event | category | flops | bytes accessed | tf_op | source)
XLA Modules:
  0.0 113.2 jit_solution(4218170200153342601)
XLA Ops:
  0.6 0.0 copy-start
  0.6 1.3 %broadcast_in_dim.2.rate_ref = f32[8,1024]{1,0:T(8,128)} broadcast(f32[1024]{0:T(1024)} %param.15), dimensions={1} | broadcast | bytes 36864 | tf_op jit(solution)/shard_map/broadcast_in_dim | solution.py:395
  2.0 1.6 %convert_element_type.36.filter_ref = bf16[64,1024]{1,0:T(8,128)(2,1)} convert(f32[64,1024]{1,0:T(8,128)} %param.14) | non-fusion elementwise | flops 65536 | bytes 393216 | tf_op jit(solution)/shard_map/convert_element_type | solution.py:395
  3.6 0.0 copy-done
  3.6 1.6 %fusion.2 = (f32[512,64]{0,1:T(8,128)S(1)}, bf16[512,64]{0,1:T(8,128)(2,1)S(1)}) fusion(f32[32,512]{1,0:T(8,128)} %constant.4.clone.feat_ref, f32[32,64]{1,0:T(8,128)S(1)} %copy-done), kind=kOutput, calls=%fused_computation.6 | convolution fusion | flops 12615680 | bytes 270336 | tf_op jit(solution)/shard_map/dot_general | solution.py:34
  5.2 0.0 copy-start.4
  5.2 0.8 copy.18.cos_ref
  6.0 0.8 copy.17.hidden_ref
  6.8 0.0 copy-done.4
  6.8 0.0 copy-start.1
  6.8 0.0 copy-start.2
  6.8 0.0 copy-start.3
  6.8 98.8 %shard_map.136 = (bf16[2,128,4096]{2,1,0:T(8,128)(2,1)}, f32[72,1024]{1,0:T(8,128)}, f32[32,64]{1,0:T(8,128)}) custom-call(bf16[128,4096]{1,0:T(8,128)(2,1)} %bitcast.13, bf16[128,4096]{1,0:T(8,128)(2,1)} %bitcast.8, bf16[128,4096]{1,0:T(8,128)(2,1)} %bitcast.9, bf16[128,4096]{1,0:T(8,128)(2,1)} %bitcast.10, bf16[512,64]{1,0:T(8,128)(2,1)} %copy.17.hidden_ref, ...), custom_call_target="tpu_custom_call" | custom-call | flops 10000000000 | bytes 10000000 | tf_op jit(solution)/shard_map/pallas_call | solution.py:350
  105.6 1.4 %slice.15 = f32[1,1024]{1,0:T(1,128)} slice(f32[72,1024]{1,0:T(8,128)} %get-tuple-element.10), slice={[64:65], [0:1024]} | slice | bytes 8192 | tf_op jit(solution)/shard_map/slice | solution.py:401
  106.9 1.7 %slice.14 = f32[64,1024]{1,0:T(8,128)} slice(f32[72,1024]{1,0:T(8,128)} %get-tuple-element.10), slice={[0:64], [0:1024]} | slice | bytes 524288 | tf_op jit(solution)/shard_map/slice | solution.py:401
  108.6 0.0 copy-done.1
  108.6 0.0 copy-done.2
  108.6 0.0 copy-done.3
  108.6 0.0 copy-start.5
  108.6 4.0 %fusion.1 = (bf16[1,128,4096]{2,1,0:T(8,128)(2,1)}, bf16[1,128,4096]{2,1,0:T(8,128)(2,1)}, bf16[1,128,4096]{2,1,0:T(8,128)(2,1)}) fusion(bf16[1,128,4096]{2,1,0:T(8,128)(2,1)S(1)} %copy-done.1, bf16[2,128,4096]{2,1,0:T(8,128)(2,1)} %get-tuple-element.9, bf16[1,128,4096]{2,1,0:T(8,128)(2,1)S(1)} %copy-done.2, bf16[1,128,4096]{2,1,0:T(8,128)(2,1)S(1)} %copy-done.3), kind=kLoop, calls=%fused_computation.3 | loop fusion | flops 5767168 | bytes 8388608 | tf_op jit(solution)/shard_map/convert_element_type | solution.py:400
  112.6 0.0 copy-done.5
  112.6 0.6 copy.20
Async XLA Ops:
  0.6 2.9 %copy-start = (f32[32,64]{1,0:T(8,128)S(1)}, f32[32,64]{1,0:T(8,128)}, u32[]{:S(2)}) copy-start(f32[32,64]{1,0:T(8,128)} %param.13) | copy-start | bytes 24580
  5.2 1.6 %copy-start.4 = (bf16[512,64]{0,1:T(8,128)(2,1)}, bf16[512,64]{0,1:T(8,128)(2,1)S(1)}, u32[]{:S(2)}) copy-start(bf16[512,64]{0,1:T(8,128)(2,1)S(1)} %get-tuple-element.16) | copy-start | bytes 196612
  6.8 101.8 %copy-start.1 = (bf16[1,128,4096]{2,1,0:T(8,128)(2,1)S(1)}, bf16[1,128,4096]{2,1,0:T(8,128)(2,1)}, u32[]{:S(2)}) copy-start(bf16[1,128,4096]{2,1,0:T(8,128)(2,1)} %param.10) | copy-start | bytes 3145732
  6.8 101.8 %copy-start.2 = (bf16[1,128,4096]{2,1,0:T(8,128)(2,1)S(1)}, bf16[1,128,4096]{2,1,0:T(8,128)(2,1)}, u32[]{:S(2)}) copy-start(bf16[1,128,4096]{2,1,0:T(8,128)(2,1)} %param.11) | copy-start | bytes 3145732
  6.8 101.8 %copy-start.3 = (bf16[1,128,4096]{2,1,0:T(8,128)(2,1)S(1)}, bf16[1,128,4096]{2,1,0:T(8,128)(2,1)}, u32[]{:S(2)}) copy-start(bf16[1,128,4096]{2,1,0:T(8,128)(2,1)} %param.12) | copy-start | bytes 3145732
  108.6 4.0 %copy-start.5 = (f32[32,64]{1,0:T(8,128)S(1)}, f32[32,64]{1,0:T(8,128)}, u32[]{:S(2)}) copy-start(f32[32,64]{1,0:T(8,128)} %get-tuple-element.28) | copy-start | bytes 24580

commit v3 on v2

--- a/solution.py
+++ b/solution.py
@@ -42,13 +42,15 @@
     return index + bit - 2 * bit * (lax.rem(lax.div(index, bit), 2))
 
 
-def kernel(sizes, tile, q_ref, k_ref, v_ref, g_ref, hidden_ref, hidden_t_ref, cos_ref, feat_ref,
-           filter_ref, rate_ref, fwd_ref, conv_ref, grad_ref, embed_ref,
+def kernel(sizes, tile, q_ref, k_ref, v_ref, g_ref, embed_in, feat_ref, filter_in, rate_in, fwd_ref,
+           conv_ref, grad_ref, grate_ref, embed_ref,
+           filter_ref, rate_ref, hidden_ref, hidden_t_ref, cos_ref, gs_src, gs_got, red_src, fin_all,
            inv_ref, src, a_buf, b_buf, out_buf, h_buf, taps_buf, win_buf, taps_n, corr_buf, weighted_n,
            mine_buf, other_buf, b_spec, join_1, join_2, join_3,
            filter_buf, rate_buf, hg_buf, g_sum, g_got, fin_src, fin_got, e_sum, e_got,
            in_send, in_recv, ret_send, ret_recv, own_sem, red_send, red_recv, emb_send, emb_recv,
-           par_send, par_recv, rat_send, rat_recv, fin_send, fin_recv):
+           par_send, par_recv, rat_send, rat_recv, fin_send, fin_recv,
+           gs_send, gs_recv, all_send, all_recv):
     n, dpn, chn = sizes
     half = n // 2
     rows, width = q_ref.shape
@@ -58,6 +60,7 @@
     part = group // 2
     tiles = group // tile
     hid = hidden_t_ref.shape[0]
+    stream = tiles % (2 * dpn) == 0
     me = lax.axis_index("seq")
     dp = lax.axis_index("dp")
     ch = lax.axis_index("chan")
@@ -71,11 +74,12 @@
     for o in range(1, n):
         pl.semaphore_signal(barrier, inc=1, device_id=(dp, ch, lax.rem(me + o, n)), device_id_type=MESH)
         greeted += 1
-    for bit in doubling_steps(dpn):
-        pl.semaphore_signal(barrier, inc=1, device_id=(flip(dp, bit), ch, me), device_id_type=MESH)
-        greeted += 1
-    for bit in doubling_steps(chn):
-        pl.semaphore_signal(barrier, inc=1, device_id=(dp, flip(ch, bit), me), device_id_type=MESH)
+    for o in range(1, dpn):
+        for other in ([lax.rem(me + d, n) for d in range(n)] if stream else [me]):
+            pl.semaphore_signal(barrier, inc=1, device_id=(lax.rem(dp + o, dpn), ch, other), device_id_type=MESH)
+            greeted += 1
+    for o in range(1, chn):
+        pl.semaphore_signal(barrier, inc=1, device_id=(dp, lax.rem(ch + o, chn), me), device_id_type=MESH)
         greeted += 1
     pl.semaphore_wait(barrier, greeted)
 
@@ -107,6 +111,8 @@
             for source, target, send, recv in (
                 (filter_ref, filter_buf, par_send, par_recv), (rate_ref, rate_buf, rat_send, rat_recv))]
 
+    filter_ref[...] = filter_in[...].astype(NARROW)
+    rate_ref[...] = jnp.broadcast_to(rate_in[...], rate_ref.shape)
     for j in (0, 1):
         @pl.when(pair + j * half != me)
         def _():
@@ -162,12 +168,40 @@
         a_buf[up, my_rows, tcol(t)] = src[0, :, c]
         b_buf[my_rows, tcol(t)] = src[1, :, c]
 
+    each = max(1, tiles // (2 * dpn))
+
+    def gs_dest(t):
+        return lax.div(lax.rem(t, tiles // 2), each), ch, 2 * slot + lax.div(t, tiles // 2)
+
+    def gs_place(t):
+        return lax.rem(lax.rem(t, tiles // 2), each)
+
+    def gs_copy(t):
+        return pltpu.make_async_remote_copy(
+            src_ref=gs_src.at[t], dst_ref=gs_got.at[gs_place(t), 2 * dp + up], send_sem=gs_send.at[t],
+            recv_sem=gs_recv.at[gs_place(t), 2 * dp + up], device_id=gs_dest(t), device_id_type=MESH)
+
+    def gs_arrival(i, c):
+        return pltpu.make_async_remote_copy(
+            src_ref=gs_src.at[0], dst_ref=gs_got.at[i, c], send_sem=gs_send.at[0],
+            recv_sem=gs_recv.at[i, c], device_id=(dp, ch, lax.rem(me + 1, n)), device_id_type=MESH)
+
+    def all_copy(i, o):
+        return pltpu.make_async_remote_copy(
+            src_ref=red_src.at[i], dst_ref=fin_all.at[:, tcol(dp * each + i)], send_sem=all_send.at[i, o],
+            recv_sem=all_recv.at[i, o], device_id=(lax.rem(dp + o, dpn), ch, me), device_id_type=MESH)
+
     sign = (2 * up - 1).astype(WIDE)
     scale = 1.0 / (length * math.sqrt(dpn * length))
     time_scale = 1.0 / math.sqrt(length)
     hg_buf[...] = jnp.zeros_like(hg_buf)
     for i in (0, 1):
         inv_ref[i] = fwd_ref[i].T
+    pre_t = dot(embed_in[...], feat_ref[...], ((0,), (0,)), HIGHEST)
+    hidden_t = jnp.sin(pre_t)
+    hidden_t_ref[...] = hidden_t.astype(NARROW)
+    hidden_ref[...] = hidden_t.T.astype(NARROW)
+    cos_ref[...] = jnp.cos(pre_t).T
     for e in (0, 1):
         @pl.when(2 * slot + e != me)
         def _():
@@ -246,33 +280,74 @@
             return rate + jnp.sum(places(i) * taps_buf[r, tc] * corr, axis=0, keepdims=True)
 
         rate = lax.fori_loop(0, length // step, finish, jnp.zeros((1, tile), WIDE))
-        g_sum[0, 0:hid, tc] = dot(hidden_t_ref[...], weighted_n[...]) * time_scale
-        g_sum[0, hid:hid + 8, tc] = jnp.broadcast_to(rate * -time_scale, (8, tile))
+        grad = dot(hidden_t_ref[...], weighted_n[...]) * time_scale
+        rate = rate * -time_scale
+        if stream:
+            gs_src[t, 0:hid] = grad.astype(NARROW)
+            gs_src[t, hid:hid + 16] = jnp.broadcast_to(rate, (16, tile)).astype(NARROW)
+            mine = jnp.logical_and(gs_dest(t)[0] == dp, gs_dest(t)[2] == me)
+
+            @pl.when(jnp.logical_not(mine))
+            def _():
+                gs_copy(t).start()
+
+            @pl.when(mine)
+            def _():
+                gs_got[gs_place(t), 2 * dp + up] = gs_src[t]
+        else:
+            g_sum[0, 0:hid, tc] = grad
+            g_sum[0, hid:hid + 8, tc] = jnp.broadcast_to(rate, (8, tile))
         hg_buf[...] += dot(weighted_n[...], pick(filter_buf, t), ((1,), (1,)))
 
-    def exchange_embed(i, dest):
-        copy = pltpu.make_async_remote_copy(
-            src_ref=e_sum.at[i], dst_ref=e_got.at[i], send_sem=emb_send.at[i],
-            recv_sem=emb_recv.at[i], device_id=dest, device_id_type=MESH)
-        copy.start()
-        return copy
+    e_sum[0] = dot(feat_ref[...], hg_buf[...] * cos_ref[...], precision=HIGHEST) * time_scale
+
+    def embed_round(axis, base, size, index, dest):
+        def copy(o):
+            return pltpu.make_async_remote_copy(
+                src_ref=e_sum.at[axis], dst_ref=e_got.at[base + index], send_sem=emb_send.at[base + o],
+                recv_sem=emb_recv.at[base + o], device_id=dest(lax.rem(index + o, size)), device_id_type=MESH)
+
+        e_got[base + index] = e_sum[axis]
+        for o in range(1, size):
+            copy(o).start()
+        for o in range(1, size):
+            copy(o).wait()
+        total = e_got[base]
+        for o in range(1, size):
+            total = total + e_got[base + o]
+        e_sum[axis + 1] = total
+
+    embed_round(0, 0, dpn, dp, lambda at: (at, ch, me))
+    embed_round(1, dpn, chn, ch, lambda at: (dp, at, me))
+
+    if stream:
+        for i in range(each):
+            total = jnp.zeros((hid + 8, tile), WIDE)
+            for c in range(2 * dpn):
+                mine = jnp.logical_and(dp == c // 2, (c % 2) * half + pair == me)
+
+                @pl.when(jnp.logical_not(mine))
+                def _():
+                    gs_arrival(i, c).wait_recv()
+
+                total = total + gs_got[i, c].astype(WIDE)[:hid + 8]
+            red_src[i] = total
+            for o in range(1, dpn):
+                all_copy(i, o).start()
+            fin_all[:, tcol(dp * each + i)] = total
 
     i = 0
-    for bit in doubling_steps(dpn):
-        dest = (flip(dp, bit), ch, me)
+    for bit in ([] if stream else doubling_steps(dpn)):
         copy = pltpu.make_async_remote_copy(
             src_ref=g_sum.at[i], dst_ref=g_got.at[i], send_sem=red_send.at[i],
-            recv_sem=red_recv.at[i], device_id=dest, device_id_type=MESH)
+            recv_sem=red_recv.at[i], device_id=(flip(dp, bit), ch, me), device_id_type=MESH)
         copy.start()
-        if i == 0:
-            e_sum[0] = dot(feat_ref[...], hg_buf[...] * cos_ref[...], precision=HIGHEST) * time_scale
-        exchange_embed(i, dest).wait()
-        e_sum[i + 1] = e_sum[i] + e_got[i]
         copy.wait()
         g_sum[i + 1] = g_sum[i] + g_got[i]
         i += 1
 
-    for e in (0, 1):
+    owners = () if stream else (0, 1)
+    for e in owners:
         fin_src[e] = g_sum[i, :, e * part:(e + 1) * part]
 
     def fin_copy(e):
@@ -285,7 +360,7 @@
             src_ref=fin_src.at[0], dst_ref=fin_got.at[j], send_sem=fin_send.at[0],
             recv_sem=fin_recv.at[j], device_id=(dp, ch, lax.rem(me + 1, n)), device_id_type=MESH)
 
-    for e in (0, 1):
+    for e in owners:
         @pl.when(2 * slot + e != me)
         def _():
             fin_copy(e).start()
@@ -294,25 +369,30 @@
         def _():
             fin_got[up] = fin_src[e]
 
-    dests = [(dp, flip(ch, bit), me) for bit in doubling_steps(chn)]
-    dests += [(dp, ch, flip(me, bit)) for bit in doubling_steps(n)]
-    for dest in dests:
-        exchange_embed(i, dest).wait()
-        e_sum[i + 1] = e_sum[i] + e_got[i]
-        i += 1
-    embed_ref[...] = e_sum[i]
+    embed_round(2, dpn + chn, n, me, lambda at: (dp, ch, at))
+    embed_ref[...] = e_sum[3]
 
     for j in (0, 1):
         @pl.when(pair + j * half != me)
         def _():
-            fin_arrival(j).wait_recv()
             for copy in par_copies(j):
                 copy.wait_send()
-    for e in (0, 1):
+    for j in owners:
+        @pl.when(pair + j * half != me)
+        def _():
+            fin_arrival(j).wait_recv()
+    for e in owners:
         @pl.when(2 * slot + e != me)
         def _():
             fin_copy(e).wait_send()
-    grad_ref[...] = fin_got[0] + fin_got[1]
+    if stream:
+        for i in range(each):
+            for o in range(1, dpn):
+                all_copy(i, o).wait()
+    else:
+        fin_all[...] = fin_got[0] + fin_got[1]
+    grad_ref[...] = fin_all[0:hid]
+    grate_ref[...] = fin_all[hid:hid + 8]
 
     @pl.loop(0, tiles)
     def _(t):
@@ -324,6 +404,10 @@
                     own_copy(t, j).wait()
             for kind in in_kinds(o):
                 in_copy(t, o, kind).wait_send()
+        if stream:
+            @pl.when(jnp.logical_not(jnp.logical_and(gs_dest(t)[0] == dp, gs_dest(t)[2] == me)))
+            def _():
+                gs_copy(t).wait_send()
 
 
 def per_device(query_input, key_input, value_input, grad_output, w_embed, w_filter, decay_rates):
@@ -339,22 +423,31 @@
     emb, hid = w_embed.shape
 
     features = jnp.asarray(embed_features(length, emb))
-    pre = dot(features, w_embed, ((0,), (0,)), HIGHEST)
-    hidden = jnp.sin(pre)
     forward = dft_tables(length)
 
     vmem = pl.BlockSpec(memory_space=pltpu.VMEM)
     dma = pltpu.SemaphoreType.DMA
     dp_steps = len(doubling_steps(dpn))
-    steps = dp_steps + len(doubling_steps(chn)) + len(doubling_steps(n))
-    conv, partial, grad_embed = pl.pallas_call(
+    members = dpn + chn + n
+    each = max(1, tiles // (2 * dpn))
+    conv, grad_filter, grad_rate, grad_embed = pl.pallas_call(
         functools.partial(kernel, (n, dpn, chn), tile),
         out_shape=(jax.ShapeDtypeStruct((2, rows, width), NARROW),
-                   jax.ShapeDtypeStruct((hid + 8, part), WIDE),
+                   jax.ShapeDtypeStruct((hid, part), WIDE),
+                   jax.ShapeDtypeStruct((8, part), WIDE),
                    jax.ShapeDtypeStruct((emb, hid), WIDE)),
-        in_specs=[vmem] * 11,
-        out_specs=(pl.BlockSpec(memory_space=pl.ANY), vmem, vmem),
+        in_specs=[vmem] * 9,
+        out_specs=(pl.BlockSpec(memory_space=pl.ANY), vmem, vmem, vmem),
         scratch_shapes=[
+            pltpu.VMEM((hid, part), NARROW),
+            pltpu.VMEM((8, part), WIDE),
+            pltpu.VMEM((length, hid), NARROW),
+            pltpu.VMEM((hid, length), NARROW),
+            pltpu.VMEM((length, hid), WIDE),
+            pltpu.VMEM((tiles, hid + 16, tile), NARROW),
+            pltpu.VMEM((each, 2 * dpn, hid + 16, tile), NARROW),
+            pltpu.VMEM((each, hid + 8, tile), WIDE),
+            pltpu.VMEM((hid + 8, part), WIDE),
             pltpu.VMEM((2, span, 2 * length), NARROW),
             pltpu.VMEM((2, rows, width), NARROW),
             pltpu.VMEM((2, span, group), NARROW),
@@ -379,26 +472,26 @@
             pltpu.VMEM((dp_steps, hid + 8, group), WIDE),
             pltpu.VMEM((2, hid + 8, part), WIDE),
             pltpu.VMEM((2, hid + 8, part), WIDE),
-            pltpu.VMEM((steps + 1, emb, hid), WIDE),
-            pltpu.VMEM((steps, emb, hid), WIDE),
+            pltpu.VMEM((4, emb, hid), WIDE),
+            pltpu.VMEM((members, emb, hid), WIDE),
             dma((tiles, half, 3)), dma((tiles, half, 3)),
             dma((tiles, half, 2)), dma((tiles, half, 2)), dma((tiles, 2)),
             dma((dp_steps,)), dma((dp_steps,)),
-            dma((steps,)), dma((steps,)),
+            dma((members,)), dma((members,)),
             dma((2,)), dma((2,)), dma((2,)), dma((2,)), dma((2,)), dma((2,)),
+            dma((tiles,)), dma((each, 2 * dpn)), dma((each, dpn)), dma((each, dpn)),
         ],
         compiler_params=pltpu.CompilerParams(
             collective_id=0, has_side_effects=True, vmem_limit_bytes=60 * 1024 * 1024),
         cost_estimate=pl.CostEstimate(flops=10**10, bytes_accessed=10**7, transcendentals=10**6),
     )(query_input[0], key_input[0], value_input[0], grad_output[0],
-      hidden.astype(NARROW), hidden.T.astype(NARROW), jnp.cos(pre), features,
-      w_filter.astype(NARROW), jnp.broadcast_to(decay_rates[None, :], (8, part)), forward)
+      w_embed, features, w_filter, decay_rates[None, :], forward)
 
     conv_out, conv_grad = conv[0:1].astype(WIDE), conv[1:2].astype(WIDE)
     d_query = (grad_output.astype(WIDE) * conv_out).astype(NARROW)
     d_key = (conv_grad * value_input.astype(WIDE)).astype(NARROW)
     d_value = (conv_grad * key_input.astype(WIDE)).astype(NARROW)
-    return (d_query, d_key, d_value, partial[:hid], partial[hid], grad_embed)
+    return (d_query, d_key, d_value, grad_filter, grad_rate[0], grad_embed)
 
 
 def solution(mesh):

time: 114 us -> 98.5 us (0.86)
  the two profiles are of different devices: /device:TPU:0 before, /device:TPU:9 now
where the time goes in v3:
time: 98.5 us; the launch traced here: 98.3 us
  Pallas kernels  90.9 us (92%)
  other arithmetic  4.03 us (4%)
  local copies, waits for them, and re-layouts  2.68 us (3%)
    pallas_call x1, Pallas kernels, per_device(): pl.pallas_call(functools.partial(kernel, (n, dpn, chn), tile), out_shape=...  90.9 us
    convert_element_type x1, other arithmetic, per_device(): d_value = (conv_grad * key_input.astype(WIDE)).astype(NARROW)  4.03 us

profile of v3, /device:TPU:9, one launch (start us, length us, event | category | flops | bytes accessed | tf_op | source)
XLA Modules:
  0.0 98.3 jit_solution(3346102212536145953)
XLA Ops:
  0.6 0.0 copy-start
  0.6 0.0 copy-start.1
  0.7 0.0 copy-start.2
  0.7 90.9 %shard_map.136 = (bf16[2,128,4096]{2,1,0:T(8,128)(2,1)}, f32[64,1024]{1,0:T(8,128)}, f32[8,1024]{1,0:T(8,128)}, f32[32,64]{1,0:T(8,128)}) custom-call(bf16[128,4096]{1,0:T(8,128)(2,1)} %bitcast.10, bf16[128,4096]{1,0:T(8,128)(2,1)} %bitcast.6, bf16[128,4096]{1,0:T(8,128)(2,1)} %bitcast.7, bf16[128,4096]{1,0:T(8,128)(2,1)} %bitcast.8, f32[32,64]{1,0:T(8,128)} %embed_in.1, ...), custom_call_target="tpu_custom_call" | custom-call | flops 10000000000 | bytes 10000000 | tf_op jit(solution)/shard_map/pallas_call | solution.py:433
  91.6 1.4 %slice.11 = f32[1,1024]{1,0:T(1,128)} slice(f32[8,1024]{1,0:T(8,128)} %get-tuple-element.12), slice={[0:1], [0:1024]} | slice | bytes 8192 | tf_op jit(solution)/shard_map/slice | solution.py:494
  92.9 0.0 copy-done
  93.0 0.0 copy-done.1
  93.0 0.0 copy-done.2
  93.0 0.0 copy-start.3
  93.0 0.0 copy-start.4
  93.0 4.0 %fusion.1 = (bf16[1,128,4096]{2,1,0:T(8,128)(2,1)}, bf16[1,128,4096]{2,1,0:T(8,128)(2,1)}, bf16[1,128,4096]{2,1,0:T(8,128)(2,1)}) fusion(bf16[1,128,4096]{2,1,0:T(8,128)(2,1)S(1)} %copy-done, bf16[2,128,4096]{2,1,0:T(8,128)(2,1)} %get-tuple-element.10, bf16[1,128,4096]{2,1,0:T(8,128)(2,1)S(1)} %copy-done.1, bf16[1,128,4096]{2,1,0:T(8,128)(2,1)S(1)} %copy-done.2), kind=kLoop, calls=%fused_computation.3 | loop fusion | flops 5767168 | bytes 8388608 | tf_op jit(solution)/shard_map/convert_element_type | solution.py:493
  97.0 0.0 copy-done.3
  97.0 0.7 copy.17
  97.7 0.0 copy-done.4
  97.7 0.6 copy.18
Async XLA Ops:
  0.6 92.3 %copy-start = (bf16[1,128,4096]{2,1,0:T(8,128)(2,1)S(1)}, bf16[1,128,4096]{2,1,0:T(8,128)(2,1)}, u32[]{:S(2)}) copy-start(bf16[1,128,4096]{2,1,0:T(8,128)(2,1)} %param.10) | copy-start | bytes 3145732
  0.6 92.3 %copy-start.1 = (bf16[1,128,4096]{2,1,0:T(8,128)(2,1)S(1)}, bf16[1,128,4096]{2,1,0:T(8,128)(2,1)}, u32[]{:S(2)}) copy-start(bf16[1,128,4096]{2,1,0:T(8,128)(2,1)} %param.11) | copy-start | bytes 3145732
  0.7 92.3 %copy-start.2 = (bf16[1,128,4096]{2,1,0:T(8,128)(2,1)S(1)}, bf16[1,128,4096]{2,1,0:T(8,128)(2,1)}, u32[]{:S(2)}) copy-start(bf16[1,128,4096]{2,1,0:T(8,128)(2,1)} %param.12) | copy-start | bytes 3145732
  93.0 4.1 %copy-start.3 = (f32[64,1024]{1,0:T(8,128)S(1)}, f32[64,1024]{1,0:T(8,128)}, u32[]{:S(2)}) copy-start(f32[64,1024]{1,0:T(8,128)} %get-tuple-element.26) | copy-start | bytes 786436
  93.0 4.8 %copy-start.4 = (f32[32,64]{1,0:T(8,128)S(1)}, f32[32,64]{1,0:T(8,128)}, u32[]{:S(2)}) copy-start(f32[32,64]{1,0:T(8,128)} %get-tuple-element.28) | copy-start | bytes 24580

commit v4 on v3

--- a/solution.py
+++ b/solution.py
@@ -194,6 +194,7 @@
     sign = (2 * up - 1).astype(WIDE)
     scale = 1.0 / (length * math.sqrt(dpn * length))
     time_scale = 1.0 / math.sqrt(length)
+    hold = max(0, tiles - 2)
     hg_buf[...] = jnp.zeros_like(hg_buf)
     for i in (0, 1):
         inv_ref[i] = fwd_ref[i].T
@@ -243,6 +244,15 @@
         for o in range(half):
             for kind in in_kinds(o):
                 in_copy(t, o, kind).wait_recv()
+
+        @pl.when(t == hold)
+        def _():
+            @pl.loop(0, hold)
+            def _(early):
+                for o in range(1, half):
+                    for j in (0, 1):
+                        ret_copy(early, o, j).start()
+
         b_spec[...] = dot(fwd_ref[up], b_buf[:, tc])
         mine_buf[...] = dot(fwd_ref[up], a_buf[up, :, tc])
         other_buf[...] = dot(fwd_ref[1 - up], a_buf[1 - up, :, tc])
@@ -265,11 +275,15 @@
 
         out_buf[0, :, tc] = dot(inv_ref[up], join_1[...]).astype(NARROW)
         out_buf[1, :, tc] = dot(inv_ref[up], join_2[...]).astype(NARROW)
-        for o in range(1, half):
-            for j in (0, 1):
-                ret_copy(t, o, j).start()
         for j in (0, 1):
             own_copy(t, j).start()
+
+        @pl.when(t >= hold)
+        def _():
+            for o in range(1, half):
+                for j in (0, 1):
+                    ret_copy(t, o, j).start()
+
         for i in (0, 1):
             corr_buf[i * span:(i + 1) * span] = dot(inv_ref[i], join_3[...])
 

time: 98.5 us -> 98.9 us (level)
  the two profiles are of different devices: /device:TPU:9 before, /device:TPU:0 now
where the time goes in v4:
time: 98.9 us; the launch traced here: 97.3 us
  Pallas kernels  89.9 us (91%)
  other arithmetic  4.03 us (4%)
  local copies, waits for them, and re-layouts  2.68 us (3%)
    pallas_call x1, Pallas kernels, per_device(): pl.pallas_call(functools.partial(kernel, (n, dpn, chn), tile), out_shape=...  89.9 us
    convert_element_type x1, other arithmetic, per_device(): d_value = (conv_grad * key_input.astype(WIDE)).astype(NARROW)  4.03 us

profile of v4, /device:TPU:0, one launch (start us, length us, event | category | flops | bytes accessed | tf_op | source)
XLA Modules:
  0.0 97.3 jit_solution(7816575040308799542)
XLA Ops:
  0.6 0.0 copy-start
  0.6 0.0 copy-start.1
  0.7 0.0 copy-start.2
  0.7 89.9 %shard_map.136 = (bf16[2,128,4096]{2,1,0:T(8,128)(2,1)}, f32[64,1024]{1,0:T(8,128)}, f32[8,1024]{1,0:T(8,128)}, f32[32,64]{1,0:T(8,128)}) custom-call(bf16[128,4096]{1,0:T(8,128)(2,1)} %bitcast.10, bf16[128,4096]{1,0:T(8,128)(2,1)} %bitcast.6, bf16[128,4096]{1,0:T(8,128)(2,1)} %bitcast.7, bf16[128,4096]{1,0:T(8,128)(2,1)} %bitcast.8, f32[32,64]{1,0:T(8,128)} %embed_in.1, ...), custom_call_target="tpu_custom_call" | custom-call | flops 10000000000 | bytes 10000000 | tf_op jit(solution)/shard_map/pallas_call | solution.py:447
  90.6 1.4 %slice.11 = f32[1,1024]{1,0:T(1,128)} slice(f32[8,1024]{1,0:T(8,128)} %get-tuple-element.12), slice={[0:1], [0:1024]} | slice | bytes 8192 | tf_op jit(solution)/shard_map/slice | solution.py:508
  91.9 0.0 copy-done
  91.9 0.0 copy-done.1
  91.9 0.0 copy-done.2
  91.9 0.0 copy-start.3
  91.9 0.0 copy-start.4
  91.9 4.0 %fusion.1 = (bf16[1,128,4096]{2,1,0:T(8,128)(2,1)}, bf16[1,128,4096]{2,1,0:T(8,128)(2,1)}, bf16[1,128,4096]{2,1,0:T(8,128)(2,1)}) fusion(bf16[1,128,4096]{2,1,0:T(8,128)(2,1)S(1)} %copy-done, bf16[2,128,4096]{2,1,0:T(8,128)(2,1)} %get-tuple-element.10, bf16[1,128,4096]{2,1,0:T(8,128)(2,1)S(1)} %copy-done.1, bf16[1,128,4096]{2,1,0:T(8,128)(2,1)S(1)} %copy-done.2), kind=kLoop, calls=%fused_computation.3 | loop fusion | flops 5767168 | bytes 8388608 | tf_op jit(solution)/shard_map/convert_element_type | solution.py:507
  96.0 0.0 copy-done.3
  96.0 0.7 copy.17
  96.7 0.0 copy-done.4
  96.7 0.6 copy.18
Async XLA Ops:
  0.6 91.3 %copy-start = (bf16[1,128,4096]{2,1,0:T(8,128)(2,1)S(1)}, bf16[1,128,4096]{2,1,0:T(8,128)(2,1)}, u32[]{:S(2)}) copy-start(bf16[1,128,4096]{2,1,0:T(8,128)(2,1)} %param.10) | copy-start | bytes 3145732
  0.6 91.3 %copy-start.1 = (bf16[1,128,4096]{2,1,0:T(8,128)(2,1)S(1)}, bf16[1,128,4096]{2,1,0:T(8,128)(2,1)}, u32[]{:S(2)}) copy-start(bf16[1,128,4096]{2,1,0:T(8,128)(2,1)} %param.11) | copy-start | bytes 3145732
  0.7 91.3 %copy-start.2 = (bf16[1,128,4096]{2,1,0:T(8,128)(2,1)S(1)}, bf16[1,128,4096]{2,1,0:T(8,128)(2,1)}, u32[]{:S(2)}) copy-start(bf16[1,128,4096]{2,1,0:T(8,128)(2,1)} %param.12) | copy-start | bytes 3145732
  91.9 4.1 %copy-start.3 = (f32[64,1024]{1,0:T(8,128)S(1)}, f32[64,1024]{1,0:T(8,128)}, u32[]{:S(2)}) copy-start(f32[64,1024]{1,0:T(8,128)} %get-tuple-element.26) | copy-start | bytes 786436
  91.9 4.8 %copy-start.4 = (f32[32,64]{1,0:T(8,128)S(1)}, f32[32,64]{1,0:T(8,128)}, u32[]{:S(2)}) copy-start(f32[32,64]{1,0:T(8,128)} %get-tuple-element.28) | copy-start | bytes 24580
